TPU v7x, 256 devices: a whole 4x4x8 slice. The times are simulated.
256 devices in a mesh: dp: 8 (over z_hi, x), ep: 8 (over y, core), ctx: 4 (over z_lo).
Axes of the slice: x: 4, y: 4, z: 8 (z_hi: 2, z_lo: 4; z = z_hi * 4 + z_lo), core: 2. Of those that a mesh axis runs over, the one named last changes fastest.
Arguments:
- layer_input: bfloat16 [32768, 1024], P(('dp', 'ep', 'ctx')), may hold values from -24 to 24
- gain_attn: float32 [1024], replicated, may hold values from 0.5 to 1.5
- w_query: bfloat16 [1024, 1024], replicated, may hold values from -0.1875 to 0.1875
- w_key: bfloat16 [1024, 512], replicated, may hold values from -0.1875 to 0.1875
- w_value: bfloat16 [1024, 512], replicated, may hold values from -0.1875 to 0.1875
- w_proj: bfloat16 [1024, 1024], replicated, may hold values from -1 to 1
- gain_ffn: float32 [1024], replicated, may hold values from 0.5 to 1.5
- w_router: bfloat16 [1024, 32], replicated, may hold values from -0.09375 to 0.09375
- w_expert_in: bfloat16 [32, 1024, 1024], P('ep'), may hold values from -0.1875 to 0.1875
- w_expert_out: bfloat16 [32, 512, 1024], P('ep'), may hold values from -1 to 1
- segment_ids: int32 [8, 4096], P('dp'), may hold values from 0 to 127, never falling along the last dimension, each value on 1 to 3072 neighbouring positions
- expert_ids: int32 [32768, 8], P(('dp', 'ep', 'ctx')), may hold values from 0 to 31, all different within a row
- slot_order: int32 [256, 1024], P(('dp', 'ep', 'ctx')), may hold values from 0 to 1023, each once within a row
- out_grad: bfloat16 [32768, 1024], P(('dp', 'ep', 'ctx')), may hold values from -6 to 6
Outputs:
- layer_output: bfloat16 [32768, 1024], P(('dp', 'ep', 'ctx'))
- input_grad: bfloat16 [32768, 1024], P(('dp', 'ep', 'ctx'))
- grad_gain_attn: float32 [1024], P(('dp', 'ep', 'ctx'))
- grad_query: float32 [1024, 1024], P(('dp', 'ep', 'ctx'))
- grad_key: float32 [1024, 512], P(('dp', 'ep', 'ctx'))
- grad_value: float32 [1024, 512], P(('dp', 'ep', 'ctx'))
- grad_proj: float32 [1024, 1024], P(('dp', 'ep', 'ctx'))
- grad_gain_ffn: float32 [1024], P(('dp', 'ep', 'ctx'))
- grad_router: float32 [1024, 32], P(('dp', 'ep', 'ctx'))
- grad_expert_in: float32 [32, 1024, 1024], P('ep', ('dp', 'ctx'))
- grad_expert_out: float32 [32, 512, 1024], P('ep', ('dp', 'ctx'))
Inputs may be any that keep to these rules, and one draw needn't show every extreme that they name: `segment_ids`: within a sequence the ids never fall; each document is at most 3072 tokens long and one is exactly that long. `expert_ids`: each row names 8 different experts. `slot_order`: each row holds every number below 1024 once.
All inputs are finite; a program needn't handle non-finite values.
Results may differ from a plain program's by a relative error of at most 0.025.
Values may be sent and summed in bfloat16 or wider, within the bound.
A program may use at most 192 MiB of HBM per device.

v0:
```python
from functools import partial

import jax
import jax.numpy as jnp
from jax import lax
from jax.sharding import PartitionSpec as P

H = 16
KV = 8
HD = 64
TOP = 8


EPSILON = 1e-06
PRECISE = lax.Precision.HIGHEST
MASKED = -1e30


def rms_norm(values, norm_gain):
    return (
        values * lax.rsqrt(jnp.mean(values * values, axis=-1, keepdims=True) + EPSILON) * norm_gain
    )


def rotate(values, positions):
    middle = values.shape[-1] // 2
    frequency = 10000.0 ** (-jnp.arange(middle, dtype=jnp.float32) * 2.0 / values.shape[-1])
    angles = positions.astype(jnp.float32)[:, None] * frequency[None, :]
    cosine_part = jnp.cos(angles)[:, None, :]
    sine_part = jnp.sin(angles)[:, None, :]
    leading = values[..., :middle]
    trailing = values[..., middle:]
    return jnp.concatenate(
        [
            leading * cosine_part - trailing * sine_part,
            trailing * cosine_part + leading * sine_part,
        ],
        axis=-1,
    )


def swiglu(gate_up):
    middle = gate_up.shape[-1] // 2
    gating = gate_up[..., :middle]
    return gating / (1.0 + jnp.exp(-gating)) * gate_up[..., middle:]


def head_major(flat_rows, head_count):
    return flat_rows.reshape(flat_rows.shape[0], head_count, -1).transpose(1, 0, 2)


def fetch_keys(key_rot, value_b):
    return (
        lax.all_gather(key_rot, ("ep", "ctx"), axis=0, tiled=True),
        lax.all_gather(value_b, ("ep", "ctx"), axis=0, tiled=True),
    )


def body(
    layer_input,
    gain_attn,
    w_query,
    w_key,
    w_value,
    w_proj,
    gain_ffn,
    w_router,
    w_expert_in,
    w_expert_out,
    segment_ids,
    expert_ids,
    slot_order,
    out_grad,
):
    tok_rows = layer_input.shape[0]
    seq_len = segment_ids.shape[1]
    per_group = H // KV
    scaling = HD ** (-0.5)
    offset = lax.axis_index(("ep", "ctx")) * tok_rows
    positions = offset + jnp.arange(tok_rows, dtype=jnp.int32)
    doc_ids = segment_ids[0]
    query_docs = lax.dynamic_slice_in_dim(doc_ids, offset, tok_rows)
    key_places = jnp.arange(seq_len, dtype=jnp.int32)
    allowed = (
        (positions[:, None] >= key_places[None, :])
        & (key_places[None, :] >= 0)
        & (query_docs[:, None] == doc_ids[None, :])
    )
    inputs = layer_input.astype(jnp.float32)
    normed = rms_norm(inputs, gain_attn)
    normed_b = normed.astype(jnp.bfloat16)
    query_pre = jnp.dot(normed_b, w_query, preferred_element_type=jnp.float32).reshape(
        tok_rows, H, HD
    )
    key_pre = jnp.dot(normed_b, w_key, preferred_element_type=jnp.float32).reshape(tok_rows, KV, HD)
    value_b = jnp.dot(normed_b, w_value, preferred_element_type=jnp.float32).astype(jnp.bfloat16)
    rope_fixed = partial(rotate, positions=positions)
    query_rot = rope_fixed(query_pre).astype(jnp.bfloat16)
    key_rot = rope_fixed(key_pre).astype(jnp.bfloat16).reshape(tok_rows, KV * HD)
    query_groups = query_rot.reshape(tok_rows, KV, per_group, HD).transpose(1, 2, 0, 3)
    key_full, value_full = fetch_keys(key_rot, value_b)
    key_heads = head_major(key_full, KV)
    value_heads = head_major(value_full, KV)

    def forward_group(packed):
        query_grp, key_head, value_head = packed
        scores = (
            jnp.einsum("gqd,kd->gqk", query_grp, key_head, preferred_element_type=jnp.float32)
            * scaling
        )
        scores = jnp.where(allowed[None], scores, MASKED)
        maxima = jnp.max(scores, axis=-1, keepdims=True)
        exponent = jnp.exp(scores - maxima)
        totals = jnp.sum(exponent, axis=-1, keepdims=True)
        attn_probs = (exponent / totals).astype(jnp.bfloat16)
        outputs = jnp.einsum(
            "gqk,kd->gqd", attn_probs, value_head, preferred_element_type=jnp.float32
        )
        return (outputs, (maxima + jnp.log(totals))[..., 0])

    attn_heads, log_sums = lax.map(forward_group, (query_groups, key_heads, value_heads))
    attended_b = attn_heads.transpose(2, 0, 1, 3).reshape(tok_rows, H * HD).astype(jnp.bfloat16)
    mixed = jnp.dot(attended_b, w_proj, preferred_element_type=jnp.float32)
    residual = inputs + mixed
    normed_ffn = rms_norm(residual, gain_ffn)
    normed_ffn_b = normed_ffn.astype(jnp.bfloat16)
    expert_total = w_router.shape[1]
    logits = jnp.dot(normed_ffn_b, w_router, preferred_element_type=jnp.float32)
    onehot = (
        expert_ids[:, :, None] == jnp.arange(expert_total, dtype=jnp.int32)[None, None, :]
    ).astype(jnp.float32)
    chosen = jnp.einsum("tke,te->tk", onehot, logits, precision=PRECISE)
    maxima = jnp.max(chosen, axis=1, keepdims=True)
    exponent = jnp.exp(chosen - maxima)
    gate_weights = exponent / jnp.sum(exponent, axis=1, keepdims=True)
    local_experts = w_expert_in.shape[0]
    ep_count = lax.axis_size("ep")
    pair_count = tok_rows * TOP
    capacity = 5 * pair_count // (4 * expert_total)
    total_slots = expert_total * capacity
    flat_ids = expert_ids.reshape(pair_count)
    priority = slot_order[0]
    earlier = (flat_ids[:, None] == flat_ids[None, :]) & (priority[None, :] < priority[:, None])
    slot_rank = jnp.sum(earlier.astype(jnp.int32), axis=1)
    local_slot = flat_ids % local_experts
    owner_ep = flat_ids // local_experts
    slot_index = jnp.where(
        slot_rank < capacity, (local_slot * ep_count + owner_ep) * capacity + slot_rank, total_slots
    )
    slot_pair = (
        jnp.full((total_slots,), pair_count, jnp.int32)
        .at[slot_index]
        .set(jnp.arange(pair_count, dtype=jnp.int32), mode="drop")
    )
    zero_row = jnp.zeros((1, layer_input.shape[1]), jnp.bfloat16)
    padded_rows = jnp.concatenate([normed_ffn_b, zero_row], axis=0)
    outgoing = padded_rows[jnp.minimum(slot_pair // TOP, tok_rows)].reshape(
        local_experts, ep_count, capacity, -1
    )
    received = lax.all_to_all(outgoing, "ep", split_axis=1, concat_axis=1, tiled=True).reshape(
        local_experts, ep_count * capacity, -1
    )
    gate_up = jnp.einsum("erd,edf->erf", received, w_expert_in, preferred_element_type=jnp.float32)
    act_b = swiglu(gate_up).astype(jnp.bfloat16)
    expert_out = jnp.einsum(
        "erf,efd->erd", act_b, w_expert_out, preferred_element_type=jnp.float32
    ).astype(jnp.bfloat16)
    returned = lax.all_to_all(
        expert_out.reshape(local_experts, ep_count, capacity, -1),
        "ep",
        split_axis=1,
        concat_axis=1,
        tiled=True,
    )
    returned_pad = jnp.concatenate([returned.reshape(total_slots, -1), zero_row], axis=0)
    pair_out = returned_pad[slot_index].reshape(tok_rows, TOP, -1).astype(jnp.float32)
    expert_sum = jnp.einsum("tk,tkd->td", gate_weights, pair_out, precision=PRECISE)
    layer_output = (residual + expert_sum).astype(jnp.bfloat16)
    grad_out = out_grad.astype(jnp.float32)
    grad_gates = jnp.einsum("td,tkd->tk", grad_out, pair_out, precision=PRECISE)
    pair_grad = (
        (gate_weights[:, :, None] * grad_out[:, None, :])
        .astype(jnp.bfloat16)
        .reshape(pair_count, -1)
    )
    slot_grad = jnp.concatenate([pair_grad, zero_row], axis=0)[slot_pair].reshape(
        local_experts, ep_count, capacity, -1
    )
    recv_grad = lax.all_to_all(slot_grad, "ep", split_axis=1, concat_axis=1, tiled=True).reshape(
        local_experts, ep_count * capacity, -1
    )
    grad_w_out = jnp.einsum("erf,erd->efd", act_b, recv_grad, preferred_element_type=jnp.float32)
    grad_act = jnp.einsum(
        "erd,efd->erf", recv_grad, w_expert_out, preferred_element_type=jnp.float32
    )
    swiglu_out, swiglu_back = jax.vjp(swiglu, gate_up)
    grad_gate_up = swiglu_back(grad_act)[0].astype(jnp.bfloat16)
    grad_w_in = jnp.einsum(
        "erd,erf->edf", received, grad_gate_up, preferred_element_type=jnp.float32
    )
    grad_rows = jnp.einsum(
        "erf,edf->erd", grad_gate_up, w_expert_in, preferred_element_type=jnp.float32
    ).astype(jnp.bfloat16)
    back_rows = lax.all_to_all(
        grad_rows.reshape(local_experts, ep_count, capacity, -1),
        "ep",
        split_axis=1,
        concat_axis=1,
        tiled=True,
    )
    back_pad = jnp.concatenate([back_rows.reshape(total_slots, -1), zero_row], axis=0)
    grad_normed_ffn = jnp.sum(
        back_pad[slot_index].reshape(tok_rows, TOP, -1).astype(jnp.float32), axis=1
    )
    grad_chosen = gate_weights * (
        grad_gates - jnp.sum(gate_weights * grad_gates, axis=1, keepdims=True)
    )
    grad_logits = jnp.einsum("tk,tke->te", grad_chosen, onehot, precision=PRECISE)
    grad_router = jnp.dot(normed_ffn_b.astype(jnp.float32).T, grad_logits, precision=PRECISE)
    grad_normed_ffn = grad_normed_ffn + jnp.dot(
        grad_logits, w_router.astype(jnp.float32).T, precision=PRECISE
    )
    norm_two_out, norm_two_back = jax.vjp(rms_norm, residual, gain_ffn)
    grad_resid_norm, grad_gain_two = norm_two_back(grad_normed_ffn)
    grad_residual = grad_out + grad_resid_norm
    grad_mixed_b = grad_residual.astype(jnp.bfloat16)
    grad_proj = jnp.einsum(
        "ti,td->id", attended_b, grad_mixed_b, preferred_element_type=jnp.float32
    )
    grad_attended = jnp.einsum(
        "td,id->ti", grad_mixed_b, w_proj, preferred_element_type=jnp.float32
    ).astype(jnp.bfloat16)
    grad_groups = grad_attended.reshape(tok_rows, KV, per_group, HD).transpose(1, 2, 0, 3)
    key_again, value_again = fetch_keys(key_rot, value_b)
    key_heads_back = head_major(key_again, KV)
    value_heads_back = head_major(value_again, KV)

    def backward_group(packed):
        query_grp, key_head, value_head, grad_grp, log_grp = packed
        scores = (
            jnp.einsum("gqd,kd->gqk", query_grp, key_head, preferred_element_type=jnp.float32)
            * scaling
        )
        scores = jnp.where(allowed[None], scores, MASKED)
        attn_probs = jnp.exp(scores - log_grp[..., None])
        grad_probs = jnp.einsum(
            "gqd,kd->gqk", grad_grp, value_head, preferred_element_type=jnp.float32
        )
        grad_value_head = jnp.einsum(
            "gqk,gqd->kd",
            attn_probs.astype(jnp.bfloat16),
            grad_grp,
            preferred_element_type=jnp.float32,
        )
        row_dots = jnp.sum(attn_probs * grad_probs, axis=-1, keepdims=True)
        grad_scores = (attn_probs * (grad_probs - row_dots)).astype(jnp.bfloat16)
        grad_query_grp = (
            jnp.einsum("gqk,kd->gqd", grad_scores, key_head, preferred_element_type=jnp.float32)
            * scaling
        )
        grad_key_head = (
            jnp.einsum("gqk,gqd->kd", grad_scores, query_grp, preferred_element_type=jnp.float32)
            * scaling
        )
        return (grad_query_grp, grad_key_head, grad_value_head)

    grad_query_groups, grad_key_heads, grad_value_heads = lax.map(
        backward_group, (query_groups, key_heads_back, value_heads_back, grad_groups, log_sums)
    )
    key_rows = grad_key_heads.shape[1]
    grad_key_full = grad_key_heads.transpose(1, 0, 2).reshape(key_rows, KV * HD)
    grad_value_full = grad_value_heads.transpose(1, 0, 2).reshape(key_rows, KV * HD)
    grad_key_rot, grad_value_rows = (
        lax.psum_scatter(
            grad_key_full.astype(jnp.bfloat16), ("ep", "ctx"), scatter_dimension=0, tiled=True
        ).astype(jnp.float32),
        lax.psum_scatter(
            grad_value_full.astype(jnp.bfloat16), ("ep", "ctx"), scatter_dimension=0, tiled=True
        ).astype(jnp.float32),
    )
    grad_query_rot = grad_query_groups.transpose(2, 0, 1, 3).reshape(tok_rows, H, HD)
    query_unused, query_rope_back = jax.vjp(rope_fixed, query_pre)
    key_unused, key_rope_back = jax.vjp(rope_fixed, key_pre)
    grad_query_b = query_rope_back(grad_query_rot)[0].reshape(tok_rows, H * HD).astype(jnp.bfloat16)
    grad_key_b = (
        key_rope_back(grad_key_rot.reshape(tok_rows, KV, HD))[0]
        .reshape(tok_rows, KV * HD)
        .astype(jnp.bfloat16)
    )
    grad_value_b = grad_value_rows.astype(jnp.bfloat16)
    grad_query_w = jnp.einsum(
        "td,tf->df", normed_b, grad_query_b, preferred_element_type=jnp.float32
    )
    grad_key_w = jnp.einsum("td,tf->df", normed_b, grad_key_b, preferred_element_type=jnp.float32)
    grad_value_w = jnp.einsum(
        "td,tf->df", normed_b, grad_value_b, preferred_element_type=jnp.float32
    )
    grad_normed = (
        jnp.einsum("tf,df->td", grad_query_b, w_query, preferred_element_type=jnp.float32)
        + jnp.einsum("tf,df->td", grad_key_b, w_key, preferred_element_type=jnp.float32)
        + jnp.einsum("tf,df->td", grad_value_b, w_value, preferred_element_type=jnp.float32)
    )
    norm_one_out, norm_one_back = jax.vjp(rms_norm, inputs, gain_attn)
    grad_input_norm, grad_gain_one = norm_one_back(grad_normed)
    input_grad = (grad_residual + grad_input_norm).astype(jnp.bfloat16)
    dense_sums = (
        lax.psum_scatter(grad_gain_one, ("dp", "ep", "ctx"), scatter_dimension=0, tiled=True),
        lax.psum_scatter(grad_query_w, ("dp", "ep", "ctx"), scatter_dimension=0, tiled=True),
        lax.psum_scatter(grad_key_w, ("dp", "ep", "ctx"), scatter_dimension=0, tiled=True),
        lax.psum_scatter(grad_value_w, ("dp", "ep", "ctx"), scatter_dimension=0, tiled=True),
        lax.psum_scatter(grad_proj, ("dp", "ep", "ctx"), scatter_dimension=0, tiled=True),
        lax.psum_scatter(grad_gain_two, ("dp", "ep", "ctx"), scatter_dimension=0, tiled=True),
        lax.psum_scatter(grad_router, ("dp", "ep", "ctx"), scatter_dimension=0, tiled=True),
    )
    expert_sums = (
        lax.psum_scatter(
            grad_w_in.astype(jnp.bfloat16), ("dp", "ctx"), scatter_dimension=1, tiled=True
        ).astype(jnp.float32),
        lax.psum_scatter(
            grad_w_out.astype(jnp.bfloat16), ("dp", "ctx"), scatter_dimension=1, tiled=True
        ).astype(jnp.float32),
    )
    return (
        layer_output,
        input_grad,
        dense_sums[0],
        dense_sums[1],
        dense_sums[2],
        dense_sums[3],
        dense_sums[4],
        dense_sums[5],
        dense_sums[6],
        expert_sums[0],
        expert_sums[1],
    )


def solution(mesh):
    in_specs = (
        P(("dp", "ep", "ctx"), None),
        P(),
        P(),
        P(),
        P(),
        P(),
        P(),
        P(),
        P("ep", None, None),
        P("ep", None, None),
        P("dp", None),
        P(("dp", "ep", "ctx"), None),
        P(("dp", "ep", "ctx"), None),
        P(("dp", "ep", "ctx"), None),
    )
    out_specs = (
        P(("dp", "ep", "ctx"), None),
        P(("dp", "ep", "ctx"), None),
        P(("dp", "ep", "ctx")),
        P(("dp", "ep", "ctx"), None),
        P(("dp", "ep", "ctx"), None),
        P(("dp", "ep", "ctx"), None),
        P(("dp", "ep", "ctx"), None),
        P(("dp", "ep", "ctx")),
        P(("dp", "ep", "ctx"), None),
        P("ep", ("dp", "ctx"), None),
        P("ep", ("dp", "ctx"), None),
    )
    return jax.shard_map(body, mesh=mesh, in_specs=in_specs, out_specs=out_specs, check_vma=False)
```

profile of v0, /device:TPU:8, one launch (start us, length us, event | category | flops | bytes accessed | tf_op | source)
XLA Modules:
  0.0 1572.3 jit_solution(14585196784440242653)
XLA Ops:
  8.5 2.3 convolution_convert_fusion.5
  15.9 4.3 scatter_custom_fusion
  20.9 2.6 fusion.97
  23.6 79.7 %all-gather.5.cloned.1.call-done = bf16[4096,512]{1,0:T(8,128)(2,1)} async-done(((bf16[128,512]{1,0:T(8,128)(2,1)}), bf16[4096,512]{1,0:T(8,128)(2,1)}) %all-gather.5.cloned.1.call-update) | async-done | bytes 4194320 | tf_op jit(solution)/shard_map/all_gather | solution.py:55
  103.4 6.4 copy.58
  109.7 82.7 %all-gather.3.cloned.1.call-done = bf16[4096,512]{0,1:T(8,128)(2,1)} async-done(((bf16[128,512]{0,1:T(8,128)(2,1)}), bf16[4096,512]{0,1:T(8,128)(2,1)}) %all-gather.3.cloned.1.call-update) | async-done | bytes 4194320 | tf_op jit(solution)/shard_map/all_gather | solution.py:54
  192.5 47.5 %while.30 = (s32[]{:T(128)}, bf16[8,2,128,64]{2,3,1,0:T(8,128)(2,1)S(1)}, f32[8,2,128]{2,1,0:T(2,128)}, bf16[8,2,128,64]{2,3,1,0:T(8,128)(2,1)S(1)}, bf16[8,4096...) while((s32[]{:T(128)}, ...), condition=%wide.region_4.5_spmd.clone.clone, body=%wide.region_1.4_spmd.clone.sunk.clone | while | flops 278396672 | bytes 14806621 | solution.py:121
  193.0 2.1 fusion.182
  204.9 2.1 fusion.182
  210.8 2.1 fusion.182
  216.7 2.1 fusion.182
  222.7 2.1 fusion.182
  228.6 2.1 fusion.182
  234.5 2.1 fusion.182
  242.3 5.1 gather_fusion
  247.4 2.2 copy.62
  249.6 47.3 %all_to_all.20 = bf16[4,8,40,1024]{3,2,0,1:T(8,128)(2,1)S(1)} all-to-all(bf16[4,8,40,1024]{3,2,0,1:T(8,128)(2,1)S(1)} %copy.62), channel_id=1, replica_groups=mesh['dp'=8,'ep'=8,'ctx'=4] {'ep'}, dimensions={1} | all-to-all | bytes 5242880 | tf_op jit(solution)/shard_map/all_to_all | solution.py:160
  297.1 2.9 fusion.102
  307.5 5.9 all-to-all-start.1
  319.1 25.8 %all-to-all-done.1 = bf16[4,8,40,1024]{3,2,0,1:T(8,128)(2,1)} async-done(((bf16[4,8,40,1024]{3,2,0,1:T(8,128)(2,1)}), bf16[4,8,40,1024]{3,2,0,1:T(8,128)(2,1)}, u32[]{:S(2)}, u32[]{:S(2)}) %all-to-all-start.1) | async-done | bytes 2621472 | tf_op jit(solution)/shard_map/all_to_all | solution.py:168
  348.6 8.2 gather_fusion.1
  356.8 2.8 fusion.51
  363.3 8.6 gather_fusion.2
  373.9 35.7 %all_to_all.21 = bf16[4,8,40,1024]{3,2,0,1:T(8,128)(2,1)S(1)} all-to-all(bf16[4,8,40,1024]{3,2,0,1:T(8,128)(2,1)S(1)} %copy.66), channel_id=1, replica_groups=mesh['dp'=8,'ep'=8,'ctx'=4] {'ep'}, dimensions={1} | all-to-all | bytes 5242880 | tf_op jit(solution)/shard_map/all_to_all | solution.py:189
  409.8 2.9 copy-done.5
  412.7 6.1 fusion.68
  418.8 9.3 convolution_convert_fusion.2
  428.1 3.5 copy.68
  431.6 5.9 all-to-all-start.3
  440.1 4.2 fusion.53
  444.3 24.7 %all-to-all-done.3 = bf16[4,8,40,1024]{3,2,0,1:T(8,128)(2,1)} async-done(((bf16[4,8,40,1024]{3,2,0,1:T(8,128)(2,1)}), bf16[4,8,40,1024]{3,2,0,1:T(8,128)(2,1)}, u32[]{:S(2)}, u32[]{:S(2)}) %all-to-all-start.3) | async-done | bytes 2621472 | tf_op jit(solution)/shard_map/all_to_all | solution.py:204
  472.7 8.1 gather_fusion.3
  480.9 3.1 convert_reduce_fusion
  489.8 106.0 %while.31 = (s32[]{:T(128)}, f32[8,2,128,64]{2,3,1,0:T(8,128)}, bf16[8,4096,64]{1,2,0:T(8,128)(2,1)}, bf16[8,4096,64]{1,2,0:T(8,128)(2,1)}, bf16[8,2,128,64]{2,3...) while((s32[]{:T(128)}, f32[8,2,128,64]{2,3,1,0:T(8,128)}, ...), condition=%wide.region_15.16_spmd.clone.clone, body=%wide.region_13.15_spmd.clone.sunk.clone | while | flops 682376960 | bytes 36400248 | solution.py:267
  492.7 2.8 multiply_reduce_fusion.7
  500.6 2.4 fusion.196
  506.0 2.8 multiply_reduce_fusion.7
  513.8 2.4 fusion.196
  519.2 2.8 multiply_reduce_fusion.7
  527.1 2.4 fusion.196
  532.4 2.8 multiply_reduce_fusion.7
  540.3 2.4 fusion.196
  545.7 2.8 multiply_reduce_fusion.7
  553.6 2.4 fusion.196
  559.0 2.8 multiply_reduce_fusion.7
  566.8 2.4 fusion.196
  572.2 2.8 multiply_reduce_fusion.7
  580.0 2.4 fusion.196
  585.4 2.8 multiply_reduce_fusion.7
  593.3 2.4 fusion.196
  595.7 6.5 copy.81
  602.4 6.5 copy.83
  609.0 6.1 convolution_convert_fusion.1
  615.2 11.2 convolution_convert_fusion
  629.8 2.7 fusion.92
  632.5 2.7 fusion.71
  635.3 109.7 %reduce-scatter.13.cloned.1.call-done = bf16[128,512]{1,0:T(8,128)(2,1)} async-done(((bf16[4096,512]{1,0:T(8,128)(2,1)}), bf16[128,512]{1,0:T(8,128)(2,1)}) %reduce-scatter.13.cloned.1.call-update) | async-done | bytes 131088
  748.0 154.7 %reduce-scatter.15.cloned.1.call-done = bf16[128,512]{1,0:T(8,128)(2,1)} async-done(((bf16[4096,512]{1,0:T(8,128)(2,1)}), bf16[128,512]{1,0:T(8,128)(2,1)}) %reduce-scatter.15.cloned.1.call-update) | async-done | bytes 131088
  902.7 2.7 fusion.88
  905.4 3.2 fusion.103
  908.7 164.2 %reduce-scatter.11.cloned.1.call-done = bf16[4,16,1024]{2,1,0:T(8,128)(2,1)} async-done(((bf16[4,512,1024]{2,1,0:T(8,128)(2,1)}), bf16[4,16,1024]{2,1,0:T(8,128)(2,1)}) %reduce-scatter.11.cloned.1.call-update) | async-done | bytes 131088 | tf_op jit(solution)/shard_map/reduce_scatter | solution.py:319
  1077.5 76.1 %all-reduce.17 = (f32[1024]{0:T(1024)S(1)}, f32[1024]{0:T(1024)S(1)}) all-reduce(f32[1024]{0:T(1024)S(1)} %get-tuple-element.162, f32[1024]{0:T(1024)S(1)} %get-tuple-element.160), channel_id=4, replica_groups=mesh['dp'=8,'ep'=8,'ctx'=4] {'dp','ep','ctx'}, use_global_device_ids=true, to_apply=%region_20.21.clone | all-reduce | flops 2048 | bytes 16384
  1156.3 105.3 %reduce-scatter.9.cloned.1.call-done = bf16[4,32,1024]{2,1,0:T(8,128)(2,1)} async-done(((bf16[4,1024,1024]{2,1,0:T(8,128)(2,1)}), bf16[4,32,1024]{2,1,0:T(8,128)(2,1)}) %reduce-scatter.9.cloned.1.call-update) | async-done | bytes 262160 | tf_op jit(solution)/shard_map/reduce_scatter | solution.py:316
  1263.4 295.2 %all-reduce.21.cloned.1.call-done = (f32[1024,1024]{1,0:T(8,128)}, f32[1024,512]{1,0:T(8,128)}, f32[1024,512]{1,0:T(8,128)}, f32[1024,1024]{1,0:T(8,128)}, f32[1024,32]{1,0:T(8,128)}) async-done(((f32[1024,1024]{1,0:T(8,128)}, f32[1024,512]{1,0:T(8,128)}, f32[1024,512]{1,0:T(8,128)}, f32[1024,1024]{1,0:T(8,128)}, f32[1024,32]{1,0:T(8,128)}), (f32[1024,1024]{1,0:T(8,128)}, f32[1024,512]{1,0:T(8,128)}, ...) | async-done | bytes 12714000
  (287 shorter events, 163.1 us)
Async XLA Ops:
  7.2 232.9 %copy-start = (bf16[1024,1024]{1,0:T(8,128)(2,1)S(1)}, bf16[1024,1024]{1,0:T(8,128)(2,1)}, u32[]{:S(2)}) copy-start(bf16[1024,1024]{1,0:T(8,128)(2,1)} %param.23) | copy-start | bytes 6291460
  7.2 13.7 copy-start.1
  7.2 13.7 copy-start.32
  7.2 6.6 copy-start.50
  7.2 6.9 copy-start.45
  7.2 13.0 copy-start.19
  7.2 96.1 %all-gather.5.cloned.1.call-start = ((), (), s32[]{:S(2)}) async-start(), calls=%async_computation.9 | async-start | bytes 4325376 | tf_op jit(solution)/shard_map/all_gather | solution.py:55
  8.5 15.0 copy-start.52
  8.5 15.0 copy-start.43
  10.9 181.6 %all-gather.3.cloned.1.call-start = ((), (), s32[]{:S(2)}) async-start(), calls=%async_computation.8 | async-start | bytes 4325376 | tf_op jit(solution)/shard_map/all_gather | solution.py:54
  11.1 12.4 copy-start.24
  11.2 12.4 copy-start.26
  14.0 303.7 %copy-start.21 = (s32[128,8]{1,0:T(8,128)}, s32[128,8]{1,0:T(8,128)S(1)}, u32[]{:S(2)}) copy-start(s32[128,8]{1,0:T(8,128)S(1)} %copy.59) | copy-start | bytes 12292
  240.0 7.3 copy-start.17
  240.0 7.3 copy-start.34
  240.0 7.3 copy-start.36
  240.0 1.4 copy-start.38
  240.6 0.8 copy-start.6
  240.6 6.7 copy-start.53
  240.6 6.7 copy-start.48
  247.3 49.8 %slice-start = ((s8[8388608]{0:T(1024)(128)(4,1)}), s8[4194304]{0:T(1024)(128)(4,1)S(1)}, s32[]{:S(2)}) async-start(s8[8388608]{0:T(1024)(128)(4,1)} %bitcast.285), calls=%async_computation.15 | async-start | bytes 8388608
  249.5 47.6 %slice-start.1 = ((s8[8388608]{0:T(1024)(128)(4,1)}), s8[4194304]{0:T(1024)(128)(4,1)S(1)}, s32[]{:S(2)}) async-start(s8[8388608]{0:T(1024)(128)(4,1)} %bitcast.285), calls=%async_computation.16 | async-start | bytes 8388608
  297.1 2.9 copy-start.14
  300.0 2.7 copy-start.10
  300.0 4.1 copy-start.4
  307.5 9.0 copy-start.29
  307.5 37.4 %all-to-all-start.1 = ((bf16[4,8,40,1024]{3,2,0,1:T(8,128)(2,1)}), bf16[4,8,40,1024]{3,2,0,1:T(8,128)(2,1)}, u32[]{:S(2)}, u32[]{:S(2)}) async-start(bf16[4,8,40,1024]{3,2,0,1:T(8,128)(2,1)} %copy.64), calls=%async_computation.1 | async-start | bytes 5242880 | tf_op jit(solution)/shard_map/all_to_all | solution.py:168
  318.4 28.5 %copy-start.46 = (f32[128]{0:T(128)}, f32[128]{0:T(128)S(1)}, u32[]{:S(2)}) copy-start(f32[128]{0:T(128)S(1)} %reduce_max.18) | copy-start | bytes 1540
  346.9 1.7 copy-start.40
  356.8 2.8 copy-start.47
  356.8 2.9 copy-start.51
  359.6 0.7 copy-start.28
  361.8 1.5 copy-start.42
  409.6 3.1 copy-start.5
  409.8 8.9 copy-start.3
  431.6 7.2 copy-start.22
  431.6 37.3 %all-to-all-start.3 = ((bf16[4,8,40,1024]{3,2,0,1:T(8,128)(2,1)}), bf16[4,8,40,1024]{3,2,0,1:T(8,128)(2,1)}, u32[]{:S(2)}, u32[]{:S(2)}) async-start(bf16[4,8,40,1024]{3,2,0,1:T(8,128)(2,1)} %copy.68), calls=%async_computation.3 | async-start | bytes 5242880 | tf_op jit(solution)/shard_map/all_to_all | solution.py:204
  437.5 307.5 %reduce-scatter.13.cloned.1.call-start = ((), (), s32[]{:S(2)}) async-start(), calls=%async_computation.12 | async-start | bytes 4325376
  471.0 1.7 copy-start.41
  480.9 3.2 copy-start.7
  480.9 3.2 copy-start.30
  480.9 3.2 copy-start.31
  480.9 3.2 copy-start.39
  480.9 3.2 copy-start.49
  480.9 3.8 copy-start.54
  480.9 3.8 copy-start.18
  480.9 3.8 copy-start.20
  484.7 5.1 copy-start.35
  484.7 5.1 copy-start.37
  485.6 0.8 copy-start.8
  602.2 300.5 %reduce-scatter.15.cloned.1.call-start = ((), (), s32[]{:S(2)}) async-start(), calls=%async_computation.13 | async-start | bytes 4325376
  609.0 463.9 %reduce-scatter.11.cloned.1.call-start = ((), (), s32[]{:S(2)}) async-start(), calls=%async_computation.11 | async-start | bytes 4325376 | tf_op jit(solution)/shard_map/reduce_scatter | solution.py:319
  615.2 646.5 %reduce-scatter.9.cloned.1.call-start = ((), (), s32[]{:S(2)}) async-start(), calls=%async_computation.10 | async-start | bytes 8650752 | tf_op jit(solution)/shard_map/reduce_scatter | solution.py:316
  626.4 1.0 copy-start.13
  626.4 2.2 copy-start.25
  626.4 2.2 copy-start.27
  626.4 3.3 copy-start.2
  626.4 3.3 copy-start.33
  626.5 3.3 copy-start.44
  626.5 932.2 %all-reduce.21.cloned.1.call-start = ((), (), s32[]{:S(2)}) async-start(), calls=%async_computation.14 | async-start | bytes 26214400
  629.7 2.8 copy-start.9
  629.7 2.8 copy-start.16
  905.4 171.0 %copy-start.23 = (bf16[128,512]{1,0:T(8,128)(2,1)S(1)}, bf16[128,512]{1,0:T(8,128)(2,1)}, u32[]{:S(2)}) copy-start(bf16[128,512]{1,0:T(8,128)(2,1)} %reduce-scatter.15.cloned.1.call-done) | copy-start | bytes 393220
  1072.8 3.6 copy-start.11
  (2 other events, 1.4 us)
Sparse Core Ops, SparseCore 0:
  11.0 92.2 all-gather.4
  105.7 86.7 all-gather.2
  602.3 142.6 reduce-scatter.12
  747.4 155.2 reduce-scatter.14
  905.0 167.7 reduce-scatter.10
  1075.2 186.3 reduce-scatter.8
  1268.0 290.5 all-reduce.20
where the time goes:
time: 1580 us; the launch traced here: 1570 us
  waiting for transfers between devices  1040 us (66%)
  matrix products  196 us (12%)
  blocking collectives  159 us (10%)
  local copies, waits for them, and re-layouts  98.5 us (6%)
  other arithmetic  48.5 us (3%)
    unnamed x10, waiting for transfers between devices  560 us
    reduce_scatter x1, waiting for transfers between devices, body(): lax.psum_scatter(grad_w_out.astype(jnp.bfloat16), ('dp', 'ctx'), scatter_...  164 us
    reduce_scatter x1, waiting for transfers between devices, body(): lax.psum_scatter(grad_w_in.astype(jnp.bfloat16), ('dp', 'ctx'), scatter_d...  105 us
    all_gather x1, waiting for transfers between devices, fetch_keys(): lax.all_gather(key_rot, ('ep', 'ctx'), axis=0, tiled=True)  82.7 us
    all_gather x1, waiting for transfers between devices, fetch_keys(): lax.all_gather(value_b, ('ep', 'ctx'), axis=0, tiled=True)  79.7 us
    unnamed x1, blocking collectives  76.1 us
    all_to_all x1, blocking collectives, body(): lax.all_to_all(outgoing, 'ep', split_axis=1, concat_axis=1, tiled=True)  47.3 us
    all_to_all x1, blocking collectives, body(): lax.all_to_all(slot_grad, 'ep', split_axis=1, concat_axis=1, tiled=True)  35.7 us
  transfers between devices with their start and end apart: 9, of which 9 were waited for; matrix products, arithmetic and copies ran while one was open for 5% of the time, Pallas kernels for 0%

commit v1 on v0

v1 whole, which is shorter than its diff:
```python
from functools import partial

import jax
import jax.numpy as jnp
import numpy as np
from jax import lax
from jax.experimental import pallas as pl
from jax.experimental.pallas import tpu as pltpu
from jax.sharding import PartitionSpec as P

HD = 64
EPSILON = 1e-06
MASKED = -1e30
CAP = 40
TOK = 128
BIG = 4096.0
MESH = pl.DeviceIdType.MESH
F32 = jnp.float32
BF16 = jnp.bfloat16
VMEM_LIMIT = 60 * 1024 * 1024

NT = (((1,), (1,)), ((), ()))
NN = (((1,), (0,)), ((), ()))
TN = (((0,), (0,)), ((), ()))


def mm(a, b, dims=NN):
    return lax.dot_general(a, b, dims, preferred_element_type=F32)


def mm3(a, b, dims=NN):
    high = a.astype(BF16)
    low = (a - high.astype(F32)).astype(BF16)
    return mm(high, b, dims) + mm(low, b, dims)


def where_am_i():
    dp, ep, ctx = lax.axis_index("dp"), lax.axis_index("ep"), lax.axis_index("ctx")
    return dp, ep, ctx


def remote(src, dst, send, recv, device):
    return pltpu.make_async_remote_copy(
        src_ref=src, dst_ref=dst, send_sem=send, recv_sem=recv, device_id=device, device_id_type=MESH
    )


def greet(barrier, device):
    pl.semaphore_signal(barrier, inc=1, device_id=device, device_id_type=MESH)


def rotate_half(values):
    lane = lax.broadcasted_iota(jnp.int32, values.shape, 1)
    return jnp.where(lane % HD < HD // 2, pltpu.roll(values, 96, 1), pltpu.roll(values, 32, 1))


def rope_block(block, ca_ref, sa_ref, cb_ref, sb_ref):
    ca, sa = ca_ref[pl.ds(block, 1), :], sa_ref[pl.ds(block, 1), :]
    cb, sb = cb_ref[...], sb_ref[...]
    cosine = ca * cb - sa * sb
    sine = sa * cb + ca * sb
    lane = lax.broadcasted_iota(jnp.int32, cosine.shape, 1)
    return cosine, jnp.where(lane % HD < HD // 2, -sine, sine)


def rope_tables():
    frequency = 10000.0 ** (-np.arange(HD // 2, dtype=np.float64) * 2.0 / HD)
    frequency = np.tile(frequency.astype(np.float32).astype(np.float64), 4)
    blocks = np.arange(32, dtype=np.float64)[:, None] * 128.0 * frequency[None, :]
    rows = np.arange(128, dtype=np.float64)[:, None] * frequency[None, :]
    return [t.astype(np.float32) for t in (np.cos(blocks), np.sin(blocks), np.cos(rows), np.sin(rows))]


class EpGather:
    COUNT = 13

    def __init__(self, ref, send, recv, place):
        self.ref, self.send, self.recv = ref, send, recv
        dp, ep, ctx = place
        y, k = ep // 2, ep % 2
        self.up = (dp, ((y + 1) % 4) * 2 + k, ctx)
        self.dn = (dp, ((y + 3) % 4) * 2 + k, ctx)
        self.sib = (dp, y * 2 + 1 - k, ctx)

        def at(dy, other):
            return ((y + dy) % 4) * 2 + ((1 - k) if other else k)

        u, s, d = self.up, self.sib, self.dn
        self.sends = [
            (at(0, 0), None, s), (at(0, 0), 0, u), (at(0, 0), 1, u), (at(0, 0), 1, d), (at(0, 0), 0, d),
            (at(3, 0), 0, u), (at(3, 0), 0, s), (at(1, 0), 1, d), (at(1, 0), 1, s),
            (at(3, 0), 1, s), (at(1, 0), 0, s), (at(2, 0), 0, s), (at(2, 0), 1, s),
        ]
        self.gets = [
            (at(0, 1), None), (at(3, 0), 0), (at(3, 0), 1), (at(1, 0), 1), (at(1, 0), 0),
            (at(2, 0), 0), (at(3, 1), 0), (at(2, 0), 1), (at(1, 1), 1),
            (at(3, 1), 1), (at(1, 1), 0), (at(2, 1), 0), (at(2, 1), 1),
        ]

    def view(self, block, half):
        if half is None:
            return self.ref.at[block]
        rows = self.ref.shape[1] // 2
        return self.ref.at[block, pl.ds(half * rows, rows)]

    def go(self, *which):
        for i in which:
            block, half, device = self.sends[i]
            v = self.view(block, half)
            remote(v, v, self.send.at[i], self.recv.at[i], device).start()

    def got(self, *which):
        for i in which:
            v = self.view(*self.gets[i])
            remote(v, v, self.send.at[i], self.recv.at[i], self.sends[i][2]).wait_recv()

    def sent(self):
        for i in range(self.COUNT):
            block, half, device = self.sends[i]
            v = self.view(block, half)
            remote(v, v, self.send.at[i], self.recv.at[i], device).wait_send()

    def whole(self):
        self.got(1)
        self.go(5, 6)
        self.got(3)
        self.go(7, 8)
        self.got(2)
        self.go(9)
        self.got(4)
        self.go(10)
        self.got(5)
        self.go(11)
        self.got(7)
        self.go(12)
        self.got(0, 6, 8, 9, 10, 11, 12)


class EpScatterSum:
    COUNT = 8

    def __init__(self, part, cbuf, fbuf, gbuf, send, recv, place):
        self.part, self.cbuf, self.fbuf, self.gbuf = part, cbuf, fbuf, gbuf
        self.send, self.recv = send, recv
        dp, ep, ctx = place
        self.y, self.k = ep // 2, ep % 2
        y, k = self.y, self.k
        self.up = (dp, ((y + 1) % 4) * 2 + k, ctx)
        self.dn = (dp, ((y + 3) % 4) * 2 + k, ctx)
        self.sib = (dp, y * 2 + 1 - k, ctx)

    def block(self, dy, other=False):
        return ((self.y + dy) % 4) * 2 + ((1 - self.k) if other else self.k)

    def copy(self, i):
        half = self.cbuf.shape[1] // 2
        lo, hi = pl.ds(0, half), pl.ds(half, half)
        s, r = self.send, self.recv
        if i < 4:
            away = self.block((2, 1, 3, 0)[i], True)
            return remote(self.part.at[away], self.cbuf.at[i], s.at[i], r.at[i], self.sib)
        src, dst, device = (
            (self.cbuf.at[0, lo], self.fbuf.at[0], self.up),
            (self.cbuf.at[0, hi], self.fbuf.at[1], self.dn),
            (self.cbuf.at[1], self.gbuf.at[0], self.up),
            (self.cbuf.at[2], self.gbuf.at[1], self.dn),
        )[i - 4]
        return remote(src, dst, s.at[i], r.at[i], device)

    def start(self):
        for i in range(4):
            self.copy(i).start()

    def far(self):
        self.copy(0).wait_recv()
        self.cbuf[0] = (self.cbuf[0].astype(F32) + self.part[self.block(2)].astype(F32)).astype(BF16)
        self.copy(4).start()
        self.copy(5).start()

    def near(self):
        half = self.cbuf.shape[1] // 2
        for slot, dy, far, rows, rest in ((1, 1, 0, pl.ds(0, half), pl.ds(half, half)), (2, 3, 1, pl.ds(half, half), pl.ds(0, half))):
            b = self.block(dy)
            self.copy(slot).wait_recv()
            self.copy(4 + far).wait_recv()
            self.cbuf[slot, rows] = (
                self.cbuf[slot, rows].astype(F32) + self.part[b, rows].astype(F32) + self.fbuf[far].astype(F32)
            ).astype(BF16)
            self.cbuf[slot, rest] = (self.cbuf[slot, rest].astype(F32) + self.part[b, rest].astype(F32)).astype(BF16)
            self.copy(6 + far).start()

    def last(self):
        for i in (3, 6, 7):
            self.copy(i).wait_recv()
        return (
            self.part[self.block(0)].astype(F32) + self.cbuf[3].astype(F32)
            + self.gbuf[0].astype(F32) + self.gbuf[1].astype(F32)
        )

    def sent(self):
        for i in range(self.COUNT):
            self.copy(i).wait_send()


def scatter_sum_scratch():
    return [
        pltpu.VMEM((4, TOK, 1024), BF16),
        pltpu.VMEM((2, TOK // 2, 1024), BF16),
        pltpu.VMEM((2, TOK, 1024), BF16),
        pltpu.SemaphoreType.DMA((8,)),
        pltpu.SemaphoreType.DMA((8,)),
    ]


def exchange(src, dst, send, recv, place, wait):
    dp, ep, ctx = place
    for r in range(1, 8):
        to, source = (ep + r) % 8, (ep + 8 - r) % 8
        if not wait:
            remote(src.at[to], dst.at[ep], send.at[r], recv.at[r], (dp, to, ctx)).start()
        else:
            remote(src.at[to], dst.at[source], send.at[r], recv.at[r], (dp, to, ctx)).wait_recv()


def exchange_sent(src, dst, send, recv, place):
    dp, ep, ctx = place
    for r in range(1, 8):
        to = (ep + r) % 8
        remote(src.at[to], dst.at[ep], send.at[r], recv.at[r], (dp, to, ctx)).wait_send()


def starts_of(docs):
    rows = lax.broadcasted_iota(jnp.int32, docs.shape, 0)
    lane = lax.broadcasted_iota(jnp.int32, docs.shape, 1)
    docs = docs.astype(F32)
    turned = pltpu.roll(docs, 1, 1)
    before = jnp.where(lane == 0, pltpu.roll(turned, 1, 0), turned)
    place = rows * 128 + lane
    fresh = (docs != before) | (place == 0)
    value = jnp.where(fresh, place.astype(F32), 0.0)
    for shift in (1, 2, 4, 8, 16, 32, 64):
        value = jnp.maximum(value, jnp.where(lane >= shift, pltpu.roll(value, shift, 1), 0.0))
    carry = jnp.broadcast_to(jnp.max(value, axis=1, keepdims=True), value.shape)
    for shift in (1, 2, 4, 8, 16):
        carry = jnp.maximum(carry, jnp.where(rows >= shift, pltpu.roll(carry, shift, 0), 0.0))
    above = jnp.where(rows >= 1, pltpu.roll(carry, 1, 0), 0.0)
    return jnp.maximum(value, above)


def slots_of(eid_ref, eidT_ref, so_ref, soT_ref, slot_scr, sel_ref):
    def expert(index):
        return jnp.where(index % 8 < 4, (index // 8) * 4 + index % 8, -1)

    row_expert = expert(lax.broadcasted_iota(jnp.int32, (64, TOK), 0))
    lane_expert = expert(lax.broadcasted_iota(jnp.int32, (TOK, 64), 1))
    by_row = jnp.full((64, TOK), BIG, F32)
    by_lane = jnp.full((TOK, 64), BIG, F32)
    for k in range(8):
        by_row = jnp.where(eidT_ref[k : k + 1, :] == row_expert, soT_ref[k : k + 1, :].astype(F32), by_row)
        by_lane = jnp.where(eid_ref[:, k : k + 1] == lane_expert, so_ref[:, k : k + 1].astype(F32), by_lane)
    sel_ref[...] = jnp.where(by_row < BIG, 1.0, 0.0)
    for g in range(8):
        for j in range(4):
            r = 8 * g + j
            row = by_row[r : r + 1, :]
            less = jnp.where(by_lane[:, r : r + 1] < row, 1.0, 0.0)
            rank = jnp.sum(less, axis=0, keepdims=True)
            slot_scr[g, j : j + 1, :] = jnp.where((row < BIG) & (rank < CAP), rank, -1.0)
        slot_scr[g, 4:8, :] = jnp.full((4, TOK), -1.0, F32)


def first_kernel(
    x_ref, gain_ref, og_ref, w_ref, ca_ref, sa_ref, cb_ref, sb_ref, eid_ref, eidT_ref, so_ref, soT_ref, doc_ref,
    nall_ref, q_ref, kv_ref, ogall_ref, slot_ref, sel_ref, start_ref,
    slot_scr, nsend, nrecv, osend, orecv, ssend, srecv, ksend, krecv,
):
    place = where_am_i()
    dp, ep, ctx = place
    y = ep // 2
    barrier = pltpu.get_barrier_semaphore()
    for r in range(1, 8):
        greet(barrier, (dp, (ep + r) % 8, ctx))

    @pl.when(ctx > 0)
    def _():
        greet(barrier, (dp, ep, ctx - 1))

    @pl.when(ctx < 3)
    def _():
        greet(barrier, (dp, ep, ctx + 1))

    x = x_ref[...].astype(F32)
    normed = x * lax.rsqrt(jnp.mean(x * x, axis=-1, keepdims=True) + EPSILON) * gain_ref[...]
    nall_ref[ep] = normed.astype(BF16)
    ogall_ref[ep] = og_ref[...]
    edges = jnp.where(ctx > 0, 1, 0) + jnp.where(ctx < 3, 1, 0)
    pl.semaphore_wait(barrier, 7 + edges)

    gather = EpGather(nall_ref, nsend, nrecv, place)
    grads = EpGather(ogall_ref, osend, orecv, place)
    gather.go(0, 1, 3, 2, 4)

    start_ref[...] = starts_of(doc_ref[...])
    slots_of(eid_ref, eidT_ref, so_ref, soT_ref, slot_scr, sel_ref)
    slot_ref[ep] = slot_scr[ep]
    exchange(slot_scr, slot_ref, ssend, srecv, place, False)

    lane = lax.broadcasted_iota(jnp.int32, (TOK, 128), 1)

    def project(dy):
        chip = (y + dy) % 4
        rows = jnp.concatenate([nall_ref[2 * chip], nall_ref[2 * chip + 1]], axis=0)
        out = mm(rows, w_ref[...])
        for i in range(2):
            b = 2 * chip + i
            cosine, sine = rope_block(4 * b + ctx, ca_ref, sa_ref, cb_ref, sb_ref)
            q = out[i * TOK : (i + 1) * TOK, :128]
            kv = out[i * TOK : (i + 1) * TOK, 128:]
            q_rot = (q * cosine + rotate_half(q) * sine).astype(BF16)
            q_ref[b] = (q_rot.astype(F32) * (HD**-0.5)).astype(BF16)
            cosine = jnp.where(lane < HD, cosine, 1.0)
            sine = jnp.where(lane < HD, sine, 0.0)
            kv_ref[b, ctx] = (kv * cosine + rotate_half(kv) * sine).astype(BF16)

    offsets = (0, 3, 1, 2)

    def hop(direction, h, g, action):
        chip = (y + offsets[g]) % 4
        back = h - 1
        own = ctx - back if direction == 0 else ctx + back
        come = ctx - h if direction == 0 else ctx + h
        to = ctx + 1 if direction == 0 else ctx - 1
        index = (direction * 3 + back) * 4 + g
        send, recv = ksend.at[index], krecv.at[index]
        if action == "recv":
            ok = come >= 0 if direction == 0 else come <= 3

            @pl.when(ok)
            def _():
                v = kv_ref.at[pl.ds(2 * chip, 2), come]
                remote(v, v, send, recv, (dp, ep, ctx)).wait_recv()

        else:
            ok = (own >= 0) & (ctx < 3) if direction == 0 else (own <= 3) & (ctx > 0)

            @pl.when(ok)
            def _():
                v = kv_ref.at[pl.ds(2 * chip, 2), own]
                c = remote(v, v, send, recv, (dp, ep, to))
                c.start() if action == "send" else c.wait_send()

    def hops(h, g):
        for direction in (0, 1):
            if h > 1:
                hop(direction, h - 1, g, "recv")
            hop(direction, h, g, "send")

    gather.got(0)
    project(0)
    hops(1, 0)
    gather.got(1)
    gather.go(5, 6)
    gather.got(3)
    gather.go(7, 8)
    gather.got(2)
    gather.go(9)
    gather.got(4)
    gather.go(10)
    grads.go(0, 1, 3, 2, 4)
    gather.got(6, 9)
    project(3)
    hops(1, 1)
    hops(2, 0)
    gather.got(8, 10)
    project(1)
    hops(1, 2)
    hops(2, 1)
    hops(3, 0)
    gather.got(5)
    gather.go(11)
    gather.got(7)
    gather.go(12)
    gather.got(11, 12)
    project(2)
    hops(1, 3)
    hops(2, 2)
    hops(3, 1)
    hops(2, 3)
    hops(3, 2)
    grads.whole()
    hops(3, 3)
    for g in range(4):
        for direction in (0, 1):
            hop(direction, 3, g, "recv")
    exchange(slot_scr, slot_ref, ssend, srecv, place, True)
    gather.sent()
    grads.sent()
    exchange_sent(slot_scr, slot_ref, ssend, srecv, place)
    for g in range(4):
        for h in (1, 2, 3):
            for direction in (0, 1):
                hop(direction, h, g, "sent")


CHUNK = 512


def key_mask(chunk, start_row, place_row):
    keys = (lax.broadcasted_iota(jnp.int32, (CHUNK, 256), 0) + chunk * CHUNK).astype(F32)
    return (keys >= start_row) & (keys <= place_row)


def query_rows(j, ctx, start_ref):
    block = 4 * j + ctx
    start = start_ref[pl.ds(block, 1), :]
    places = (lax.broadcasted_iota(jnp.int32, (1, 128), 1) + block * 128).astype(F32)
    return jnp.concatenate([start, start], axis=1), jnp.concatenate([places, places], axis=1)


def turned(block):
    return block.astype(F32).T.astype(BF16)


def heads_wide(tall):
    return jnp.concatenate([tall[:HD], tall[HD:]], axis=1)


def attend_kernel(first_ref, q_ref, kv_ref, start_ref, att_ref, attT_ref, lse_ref, kvT):
    ctx = lax.axis_index("ctx")

    for chunk in range(8):
        part = kv_ref[chunk * CHUNK : (chunk + 1) * CHUNK, :].astype(F32).T
        row = lax.broadcasted_iota(jnp.int32, part.shape, 0)
        kvT[:, chunk * CHUNK : (chunk + 1) * CHUNK] = jnp.where(row < HD, 1.0, part).astype(BF16)

    for j in range(8):
        start_row, place_row = query_rows(j, ctx, start_ref)
        wide = heads_wide(turned(q_ref[j]))
        q_pad = jnp.concatenate([wide, jnp.zeros_like(wide)], axis=0)

        def step(chunk, carry):
            top, total = carry
            rows = pl.ds(pl.multiple_of(chunk * CHUNK, CHUNK), CHUNK)
            scores = mm(kv_ref[rows, :], q_pad)
            scores = jnp.where(key_mask(chunk, start_row, place_row), scores, MASKED)
            new_top = jnp.maximum(top, jnp.max(scores, axis=0, keepdims=True))
            probs = jnp.exp(scores - new_top).astype(BF16)
            total = total * jnp.exp(top - new_top) + mm(kvT[:, rows], probs)
            return new_top, total

        top, total = lax.fori_loop(
            first_ref[j], j + 1, step, (jnp.full((1, 256), MASKED, F32), jnp.zeros((128, 256), F32))
        )
        norm = total[0:1]
        out = total[HD:] / norm
        tall = jnp.concatenate([out[:, :128], out[:, 128:]], axis=0)
        attT_ref[j] = tall
        att_ref[j] = tall.T.astype(BF16)
        lse_ref[j] = jnp.broadcast_to(top + jnp.log(norm), (8, 256))


def attend_back_kernel(
    first_ref, q_ref, kv_ref, start_ref, attT_ref, lse_ref, gm_ref, w_ref, ca_ref, sa_ref, cb_ref, sb_ref,
    dq_ref, dkv_ref, gproj_ref, kT, acc,
):
    ctx = lax.axis_index("ctx")
    for chunk in range(8):
        part = kv_ref[chunk * CHUNK : (chunk + 1) * CHUNK, :].astype(F32).T
        kT[:, chunk * CHUNK : (chunk + 1) * CHUNK] = part[:HD].astype(BF16)
        acc[chunk * CHUNK : (chunk + 1) * CHUNK, :] = jnp.zeros((CHUNK, 128), F32)
    gproj = jnp.zeros((128, 1024), F32)
    for j in range(8):
        gproj = gproj + mm(attT_ref[j].astype(BF16), gm_ref[j])
    gproj_ref[...] = gproj
    zero = jnp.zeros((HD, 256), BF16)
    lane = lax.broadcasted_iota(jnp.int32, (256, 128), 1)
    for j in range(8):
        start_row, place_row = query_rows(j, ctx, start_ref)
        grad_tall = mm(w_ref[...], gm_ref[j], NT).astype(BF16)
        delta = jnp.sum(
            heads_wide(grad_tall.astype(F32)) * heads_wide(attT_ref[j]), axis=0, keepdims=True
        )
        q_blk = q_ref[j]
        q_pad = jnp.concatenate([heads_wide(turned(q_blk)), zero], axis=0)
        g_pad = jnp.concatenate([zero, heads_wide(grad_tall)], axis=0)
        both = jnp.concatenate([q_pad, g_pad], axis=1)
        g_blk = turned(grad_tall)
        q_f, g_f = q_blk.astype(F32), g_blk.astype(F32)
        q_rows = jnp.concatenate([q_f, pltpu.roll(q_f, HD, 1)], axis=0)
        g_rows = jnp.concatenate([pltpu.roll(g_f, HD, 1), g_f], axis=0)
        stack = jnp.concatenate(
            [jnp.where(lane < HD, q_rows, 0.0), jnp.where(lane < HD, 0.0, g_rows)], axis=0
        ).astype(BF16)
        lse = lse_ref[j, 0:1, :]

        def step(chunk, dq):
            rows = pl.ds(pl.multiple_of(chunk * CHUNK, CHUNK), CHUNK)
            pair = mm(kv_ref[rows, :], both)
            scores = jnp.where(key_mask(chunk, start_row, place_row), pair[:, :256], MASKED)
            probs = jnp.exp(scores - lse)
            grad = (probs * (pair[:, 256:] - delta)).astype(BF16)
            acc[rows, :] += mm(jnp.concatenate([grad, probs.astype(BF16)], axis=1), stack)
            return dq + mm(kT[:, rows], grad)

        dq = lax.fori_loop(first_ref[j], j + 1, step, jnp.zeros((HD, 256), F32)) * (HD**-0.5)
        dq = jnp.concatenate([dq[:, :128], dq[:, 128:]], axis=0).T
        cosine, sine = rope_block(4 * j + ctx, ca_ref, sa_ref, cb_ref, sb_ref)
        dq_ref[j] = (dq * cosine - rotate_half(dq) * sine).astype(BF16)
    for chunk in range(8):
        rows = slice(chunk * CHUNK, (chunk + 1) * CHUNK)
        dkv_ref[rows, :] = acc[rows, :].astype(BF16)


def middle_kernel(
    att_ref, x_ref, gain_ref, w_ref, wr_ref, sel_ref,
    res_ref, nf_ref, gin_ref, gates_ref,
    abuf, gscr, asend, arecv, nsend, nrecv, gsend, grecv,
):
    place = where_am_i()
    dp, ep, ctx = place
    barrier = pltpu.get_barrier_semaphore()
    for r in range(1, 8):
        greet(barrier, (dp, (ep + r) % 8, ctx))
    pl.semaphore_wait(barrier, 7)
    exchange(att_ref, abuf, asend, arecv, place, False)
    abuf[ep] = att_ref[ep]
    exchange(att_ref, abuf, asend, arecv, place, True)
    attended = jnp.concatenate([abuf[p] for p in range(8)], axis=1)
    res = x_ref[...].astype(F32) + mm(attended, w_ref[...])
    res_ref[...] = res
    normed = res * lax.rsqrt(jnp.mean(res * res, axis=-1, keepdims=True) + EPSILON) * gain_ref[...]
    normed = normed.astype(BF16)
    nf_ref[ep] = normed
    gather = EpGather(nf_ref, nsend, nrecv, place)
    gather.go(0, 1, 3, 2, 4)
    logits = mm(wr_ref[...], normed, NT)
    chosen = sel_ref[...] > 0.5
    top = jnp.max(jnp.where(chosen, logits, MASKED), axis=0, keepdims=True)
    weight = jnp.where(chosen, jnp.exp(jnp.where(chosen, logits, MASKED) - top), 0.0)
    gates = weight / jnp.sum(weight, axis=0, keepdims=True)
    gates_ref[...] = gates
    for g in range(8):
        gscr[g] = gates[8 * g : 8 * g + 8, :]
    gin_ref[ep] = gscr[ep]
    exchange(gscr, gin_ref, gsend, grecv, place, False)
    gather.whole()
    exchange(gscr, gin_ref, gsend, grecv, place, True)
    gather.sent()
    exchange_sent(gscr, gin_ref, gsend, grecv, place)
    exchange_sent(att_ref, abuf, asend, arecv, place)


def expert_kernel(
    nf_ref, og_ref, slot_ref, gate_ref, win_ref, wout_ref,
    y_ref, d_ref, dg_ref, gw_ref,
    rows_scr, grad_scr,
):
    j = pl.program_id(0)
    slot = lax.broadcasted_iota(jnp.int32, (CAP, TOK), 0).astype(F32)

    def picks(s, e):
        return slot == slot_ref[s, pl.ds(e, 1), :]

    @pl.when(j == 0)
    def _():
        def load(s, carry):
            pick = jnp.concatenate([jnp.where(picks(s, e), 1.0, 0.0) for e in range(4)], axis=0).astype(BF16)
            got = mm(pick, nf_ref[s])
            grad = mm(pick, og_ref[s])
            for e in range(4):
                rows = pl.ds(pl.multiple_of(s * CAP, 8), CAP)
                rows_scr[e, rows, :] = got[e * CAP : (e + 1) * CAP]
                grad_scr[e, rows, :] = grad[e * CAP : (e + 1) * CAP]
            return carry

        lax.fori_loop(0, 8, load, 0)

    gates = jnp.concatenate(
        [jnp.sum(jnp.where(picks(s, j), gate_ref[s, pl.ds(j, 1), :], 0.0), axis=1, keepdims=True) for s in range(8)],
        axis=0,
    )
    received = rows_scr[j].astype(BF16)
    grad_tok = grad_scr[j]
    gate_up = mm(received, win_ref[0])
    gating, up = gate_up[:, :512], gate_up[:, 512:]
    sig = 1.0 / (1.0 + jnp.exp(-gating))
    silu = gating * sig
    act = (silu * up).astype(BF16)
    result = mm(act, wout_ref[0]).astype(BF16).astype(F32)
    dots = jnp.sum(grad_tok * result, axis=1, keepdims=True)
    grad_res = (grad_tok * gates).astype(BF16)
    grad_scr[j] = result * gates
    for s in range(8):
        dg_ref[s, pl.ds(j, 1), :] = jnp.sum(
            jnp.where(picks(s, j), dots[s * CAP : (s + 1) * CAP], 0.0), axis=0, keepdims=True
        )
    gw_ref[0, :, 32:48, :] = mm(act, grad_res, TN).astype(BF16).reshape(32, 16, 1024)
    grad_act = mm(grad_res, wout_ref[0], NT)
    grad_up = (grad_act * silu).astype(BF16)
    grad_gate = (grad_act * up * sig * (1.0 + gating * (1.0 - sig))).astype(BF16)
    grad_gu = jnp.concatenate([grad_gate, grad_up], axis=1)
    gw_ref[0, :, 0:32, :] = mm(received, grad_gu, TN).astype(BF16).reshape(32, 32, 1024)
    rows_scr[j] = mm(grad_gu, win_ref[0], NT)

    @pl.when(j == 3)
    def _():
        def store(s, carry):
            pick = jnp.concatenate([jnp.where(picks(s, e), 1.0, 0.0) for e in range(4)], axis=0).astype(BF16)
            rows = pl.ds(pl.multiple_of(s * CAP, 8), CAP)
            weighted = jnp.concatenate([grad_scr[e, rows, :] for e in range(4)], axis=0).astype(BF16)
            y_ref[s] = mm(pick, weighted, TN).astype(BF16)
            back = jnp.concatenate([rows_scr[e, rows, :] for e in range(4)], axis=0).astype(BF16)
            d_ref[s] = mm(pick, back, TN).astype(BF16)
            dg_ref[s, 4:8, :] = jnp.zeros((4, TOK), F32)
            return carry

        lax.fori_loop(0, 8, store, 0)


def turn_kernel(
    part_ref, dg_ref, gates_ref, res_ref, nf_ref, og_ref, gain_ref, wr_ref,
    gm_ref, gres_ref, grouter_ref, ggain_ref,
    dbuf, cbuf, fbuf, gbuf, csend, crecv, dsend, drecv, gsend, grecv,
):
    place = where_am_i()
    dp, ep, ctx = place
    barrier = pltpu.get_barrier_semaphore()
    for r in range(1, 8):
        greet(barrier, (dp, (ep + r) % 8, ctx))
    pl.semaphore_wait(barrier, 7)
    total = EpScatterSum(part_ref, cbuf, fbuf, gbuf, csend, crecv, place)
    total.start()
    exchange(dg_ref, dbuf, dsend, drecv, place, False)
    dbuf[ep] = dg_ref[ep]
    total.far()
    total.near()
    exchange(dg_ref, dbuf, dsend, drecv, place, True)
    gates = gates_ref[...]
    grad_gates = jnp.concatenate([dbuf[p] for p in range(8)], axis=0)
    grad_logits = gates * (grad_gates - jnp.sum(gates * grad_gates, axis=0, keepdims=True))
    high = grad_logits.astype(BF16)
    low = (grad_logits - high.astype(F32)).astype(BF16)
    grouter_ref[...] = mm(high, nf_ref[...]) + mm(low, nf_ref[...])
    from_router = mm(high, wr_ref[...], TN) + mm(low, wr_ref[...], TN)
    res = res_ref[...]
    scale = lax.rsqrt(jnp.mean(res * res, axis=-1, keepdims=True) + EPSILON)
    grad_normed = total.last() + from_router
    scaled = res * scale
    ggain_ref[...] = jnp.broadcast_to(jnp.sum(grad_normed * scaled, axis=0, keepdims=True), (8, 1024))
    grad_normed = grad_normed * gain_ref[...]
    mean = jnp.mean(grad_normed * scaled, axis=-1, keepdims=True)
    gres = og_ref[...].astype(F32) + scale * (grad_normed - scaled * mean)
    gres_ref[...] = gres
    gm_ref[ep] = gres.astype(BF16)
    gather = EpGather(gm_ref, gsend, grecv, place)
    gather.go(0, 1, 3, 2, 4)
    gather.whole()
    gather.sent()
    exchange_sent(dg_ref, dbuf, dsend, drecv, place)
    total.sent()


def final_kernel(
    dq_ref, dkv_ref, part_ref, res_ref, x_ref, gain_ref, nall_ref, wq_ref, wk_ref, wv_ref, gres_ref,
    ca_ref, sa_ref, cb_ref, sb_ref, grouter_ref, ggain_ref, gproj_ref,
    out_ref, ing_ref, dense_ref,
    kbuf, dqkv, pieces, cbuf, fbuf, gbuf, csend, crecv, ksend, krecv, psend, precv,
):
    place = where_am_i()
    dp, ep, ctx = place
    barrier = pltpu.get_barrier_semaphore()
    for r in range(1, 8):
        greet(barrier, (dp, (ep + r) % 8, ctx))

    @pl.when(ctx > 0)
    def _():
        greet(barrier, (dp, ep, ctx - 1))

    @pl.when(ctx < 3)
    def _():
        greet(barrier, (dp, ep, ctx + 1))

    edges = jnp.where(ctx > 0, 1, 0) + jnp.where(ctx < 3, 1, 0)
    pl.semaphore_wait(barrier, 7 + edges)
    total = EpScatterSum(part_ref, cbuf, fbuf, gbuf, csend, crecv, place)

    def link(direction, shard, half, action):
        blocks = pl.ds(half * 4, 4)
        index = (direction * 4 + shard) * 2 + half
        send, recv = ksend.at[index], krecv.at[index]
        to = ctx + 1 if direction == 0 else ctx - 1
        first = ctx == (0 if direction == 0 else 3)
        if direction == 0:
            passes, middle, here = ctx < shard, (ctx < shard) & (ctx > 0), (ctx == shard) & (ctx > 0)
        else:
            passes, middle, here = ctx > shard, (ctx > shard) & (ctx < 3), (ctx == shard) & (ctx < 3)
        slot = kbuf.at[direction, shard, blocks]
        own = dkv_ref.at[blocks, shard]

        def copy(src):
            return remote(src, slot, send, recv, (dp, ep, to))

        if action == "send":

            @pl.when(passes & first)
            def _():
                copy(own).start()

            @pl.when(middle)
            def _():
                copy(slot).wait_recv()

                def add(b, carry):
                    b = b + half * 4
                    kbuf[direction, shard, b] = (
                        kbuf[direction, shard, b].astype(F32) + dkv_ref[b, shard].astype(F32)
                    ).astype(BF16)
                    return carry

                lax.fori_loop(0, 4, add, 0)
                copy(slot).start()

        elif action == "recv":

            @pl.when(here)
            def _():
                copy(slot).wait_recv()

        else:

            @pl.when(passes)
            def _():
                copy(slot).wait_send()

    for half in (0, 1):
        link(0, 3, half, "send")
        link(1, 0, half, "send")
    total.start()
    total.far()
    for half in (0, 1):
        link(0, 2, half, "send")
        link(1, 1, half, "send")
    for half in (0, 1):
        link(0, 1, half, "send")
        link(1, 2, half, "send")
    total.near()
    for shard in range(4):
        for half in (0, 1):
            link(0, shard, half, "recv")
            link(1, shard, half, "recv")

    lane = lax.broadcasted_iota(jnp.int32, (TOK, 128), 1)

    def own_block(b, carry):
        left = jnp.where(ctx > 0, 1.0, 0.0)
        right = jnp.where(ctx < 3, 1.0, 0.0)

        @pl.when(ctx == 0)
        def _():
            kbuf[0, 0, b] = jnp.zeros((TOK, 128), BF16)

        @pl.when(ctx == 3)
        def _():
            kbuf[1, 3, b] = jnp.zeros((TOK, 128), BF16)

        grad = dkv_ref[b, ctx].astype(F32) + kbuf[0, ctx, b].astype(F32) * left + kbuf[1, ctx, b].astype(F32) * right
        cosine, sine = rope_block(4 * b + ctx, ca_ref, sa_ref, cb_ref, sb_ref)
        cosine = jnp.where(lane < HD, cosine, 1.0)
        sine = jnp.where(lane < HD, sine, 0.0)
        dqkv[b, :, 0:128] = dq_ref[b]
        dqkv[b, :, 128:256] = (grad * cosine - rotate_half(grad) * sine).astype(BF16)
        return carry

    lax.fori_loop(0, 8, own_block, 0)
    exchange(dqkv, pieces, psend, precv, place, False)
    pieces[ep] = dqkv[ep]
    weights = mm(nall_ref[...].reshape(1024, 1024), dqkv[...].reshape(1024, 256), TN)
    dense_ref[:, :, 0:256] = weights.astype(BF16).reshape(32, 32, 256)
    gproj = gproj_ref[...].astype(BF16)
    for d in range(8):
        for c in range(4):
            dense_ref[d * 4 + c, :, 384:512] = gproj[32 * c : 32 * c + 32, 128 * d : 128 * d + 128]
    out_ref[...] = (res_ref[...] + total.last()).astype(BF16)
    exchange(dqkv, pieces, psend, precv, place, True)
    grad_q = jnp.concatenate([pieces[p, :, 0:128] for p in range(8)], axis=1)
    grad_k = jnp.concatenate([pieces[p, :, 128:192] for p in range(8)], axis=1)
    grad_v = jnp.concatenate([pieces[p, :, 192:256] for p in range(8)], axis=1)
    grad_normed = mm(grad_q, wq_ref[...], NT) + mm(grad_k, wk_ref[...], NT) + mm(grad_v, wv_ref[...], NT)
    x = x_ref[...].astype(F32)
    scale = lax.rsqrt(jnp.mean(x * x, axis=-1, keepdims=True) + EPSILON)
    scaled = x * scale
    ggain = jnp.sum(grad_normed * scaled, axis=0, keepdims=True)
    grad_normed = grad_normed * gain_ref[...]
    mean = jnp.mean(grad_normed * scaled, axis=-1, keepdims=True)
    ing_ref[...] = (gres_ref[...] + scale * (grad_normed - scaled * mean)).astype(BF16)
    side = jnp.concatenate(
        [grouter_ref[...], jnp.broadcast_to(ggain, (8, 1024)), ggain_ref[...], jnp.zeros((48, 1024), F32)], axis=0
    )
    for t in range(8):
        tile = side[:, t * 128 : (t + 1) * 128].T.astype(BF16)
        dense_ref[4 * t : 4 * t + 4, :, 256:384] = tile.reshape(4, 32, 128)
    total.sent()
    exchange_sent(dqkv, pieces, psend, precv, place)
    for shard in range(4):
        for half in (0, 1):
            for direction in (0, 1):
                link(direction, shard, half, "sent")


class Ring:
    def __init__(self, n, pos, direction, own, slots, device, send, recv, rows):
        self.n, self.pos, self.direction, self.own, self.slots = n, pos, direction, own, slots
        self.device, self.send, self.recv, self.rows = device, send, recv, rows

    def chunk(self, s):
        if self.direction > 0:
            return (self.pos + 2 * self.n - 1 - s) % self.n
        return (self.pos + 1 + s) % self.n

    def copy(self, s):
        src = self.own(self.chunk(0)) if s == 0 else self.slots.at[s - 1]
        return remote(src, self.slots.at[s], self.send.at[s], self.recv.at[s], self.device)

    def add(self, s):
        own = self.own(self.chunk(s))
        held = self.slots.at[s - 1]

        def one(i, carry):
            index = self.rows(i)
            held[index] = (held[index].astype(F32) + own[index].astype(F32)).astype(BF16)
            return carry

        lax.fori_loop(0, self.count(), one, 0)

    def count(self):
        c = 1
        for size in self.slots.shape[1:-2]:
            c *= size
        return c

    def step(self, s):
        if s > 0:
            self.copy(s - 1).wait_recv()
            self.add(s)
        self.copy(s).start()

    def sent(self):
        for s in range(self.n - 1):
            self.copy(s).wait_send()


def sums_kernel(
    gw_ref, dense_ref,
    gin_ref, gout_ref, gq_ref, gk_ref, gv_ref, gside_ref, gproj_ref,
    xa, za, zb, xb, xd, zd, ra, rb, rd, fin, rq, rp,
    xas, xar, zas, zar, zbs, zbr, xbs, xbr, xds, xdr, zds, zdr, fsend, frecv, hsend, hrecv,
):
    dp, ep, ctx = where_am_i()
    zh, x = dp // 4, dp % 4
    z = zh * 4 + ctx

    def at_x(v):
        return (zh * 4 + v % 4, ep, ctx)

    def at_z(v):
        v = v % 8
        return ((v // 4) * 4 + x, ep, v % 4)

    x_up, x_dn = at_x(x + 1), at_x(x + 3)
    z_up, z_dn = at_z(z + 1), at_z(z + 7)

    def send_to(g, h):
        return (dp, 2 * ctx + g // 2, 2 * (g % 2) + h), (ep, 2 * ctx + g // 2, 2 * (g % 2) + h)

    def is_me(device):
        return (device[0] == dp) & (device[1] == ep) & (device[2] == ctx)

    barrier = pltpu.get_barrier_semaphore()
    for device in (x_up, x_dn, z_up, z_dn):
        greet(barrier, device)
    for i in range(8):
        for device in ((dp, i, ep // 2), (i, dp, ep // 2)):

            @pl.when(jnp.logical_not(is_me(device)))
            def _():
                greet(barrier, device)

    waits = 4
    for g in range(4):
        for h in range(2):
            for device in send_to(g, h):
                waits = waits + jnp.where(is_me(device), 0, 1)
    pl.semaphore_wait(barrier, waits)

    x4 = lambda i: (i // 4, i % 4)
    z4 = lambda i: (i,)
    one = lambda i: ()

    def x_first(ref, result, slots_x, slots_z, up, sems):
        direction = 1 if up else -1
        ring_x = Ring(4, x, direction, lambda t: ref.at[:, t], slots_x, x_up if up else x_dn, sems[0], sems[1], x4)
        ring_z = Ring(8, z, direction, lambda t: result.at[t // 4, t % 4], slots_z, z_up if up else z_dn, sems[2], sems[3], one)
        return ring_x, ring_z

    def z_first(ref, result, slots_z, slots_x, up, sems):
        direction = 1 if up else -1
        ring_z = Ring(8, z, direction, lambda t: ref.at[t // 4, :, t % 4], slots_z, z_up if up else z_dn, sems[0], sems[1], z4)
        ring_x = Ring(4, x, direction, lambda t: result.at[t], slots_x, x_up if up else x_dn, sems[2], sems[3], one)
        return ring_z, ring_x

    def settle(ring, result):
        last = ring.n - 2
        ring.copy(last).wait_recv()
        own = ring.own(ring.pos)

        def each(i, carry):
            index = ring.rows(i)
            result[index] = (ring.slots.at[last][index].astype(F32) + own[index].astype(F32)).astype(BF16)
            return carry

        lax.fori_loop(0, ring.count(), each, 0)

    def finish(ring):
        last = ring.n - 2
        ring.copy(last).wait_recv()
        return ring.slots[last].astype(F32) + ring.own(ring.pos)[...].astype(F32)

    a, b, dn = [], [], []
    for i in range(2):
        a.append(x_first(gw_ref.at[i], ra.at[i], xa.at[i], za.at[i], i == 0, (xas.at[i], xar.at[i], zas.at[i], zar.at[i])))
        b.append(z_first(gw_ref.at[2 + i], rb.at[i], zb.at[i], xb.at[i], i == 0, (zbs.at[i], zbr.at[i], xbs.at[i], xbr.at[i])))
        half = dense_ref.at[:, :, :, pl.ds(16 * i, 16)]
        dn.append(x_first(half, rd.at[i], xd.at[i], zd.at[i], i == 0, (xds.at[i], xdr.at[i], zds.at[i], zdr.at[i])))

    def both(rings, which, s):
        for i in range(2):
            rings[i][which].step(s)

    both(dn, 0, 0)
    both(a, 0, 0)
    both(b, 0, 0)
    both(dn, 0, 1)
    both(dn, 0, 2)
    both(b, 0, 1)
    for i in range(2):
        settle(dn[i][0], rd.at[i])
    both(dn, 1, 0)
    both(a, 0, 1)
    both(b, 0, 2)
    both(dn, 1, 1)
    both(b, 0, 3)
    both(dn, 1, 2)
    both(a, 0, 2)
    both(dn, 1, 3)
    both(b, 0, 4)
    both(dn, 1, 4)
    both(b, 0, 5)
    both(dn, 1, 5)
    both(b, 0, 6)
    both(dn, 1, 6)

    for i in range(2):
        done = finish(dn[i][1])
        fin[2 * i] = done[0:8]
        fin[2 * i + 1] = done[8:16]

    def piece(g, h, kind, device):
        index = g * 2 + h
        if kind == 0:
            return remote(fin.at[g, :, pl.ds(0, 384)], rq.at[ep], fsend.at[index], frecv.at[ep], device)
        return remote(fin.at[g, :, pl.ds(384, 128)], rp.at[dp], hsend.at[index], hrecv.at[dp], device)

    def each_piece(act, own):
        for g in range(4):
            for h in range(2):
                for kind in (0, 1):
                    device = send_to(g, h)[kind]

                    @pl.when(jnp.logical_not(is_me(device)))
                    def _():
                        act(piece(g, h, kind, device))

                    if own:

                        @pl.when(is_me(device))
                        def _():
                            if kind == 0:
                                rq[ep] = fin[g, :, 0:384]
                            else:
                                rp[dp] = fin[g, :, 384:512]

    each_piece(lambda c: c.start(), True)

    for i in range(2):
        settle(a[i][0], ra.at[i])
    both(a, 1, 0)
    for i in range(2):
        settle(b[i][0], rb.at[i])
    both(b, 1, 0)
    both(a, 1, 1)
    both(b, 1, 1)
    both(a, 1, 2)
    both(b, 1, 2)
    both(a, 1, 3)
    for i in range(2):
        done = finish(b[i][1])
        gin_ref[2 + i] = done[0:32]
        gout_ref[2 + i] = done[32:48]
    both(a, 1, 4)
    both(a, 1, 5)
    both(a, 1, 6)

    for i in range(8):
        for kind, device in enumerate(((dp, i, ep // 2), (i, dp, ep // 2))):

            @pl.when(jnp.logical_not(is_me(device)))
            def _():
                if kind == 0:
                    src, dst, sems = fin.at[0, :, pl.ds(0, 384)], rq.at[i], (fsend.at[0], frecv.at[i])
                else:
                    src, dst, sems = fin.at[0, :, pl.ds(384, 128)], rp.at[i], (hsend.at[0], hrecv.at[i])
                remote(src, dst, sems[0], sems[1], device).wait_recv()

    odd = ctx % 2 == 1

    def mine(v):
        return jnp.where(odd, v[4:8], v[0:4])

    gq_ref[...] = mine(jnp.concatenate([rq[i, :, 0:128] for i in range(8)], axis=1))
    gk_ref[...] = mine(jnp.concatenate([rq[i, :, 128:192] for i in range(8)], axis=1))
    gv_ref[...] = mine(jnp.concatenate([rq[i, :, 192:256] for i in range(8)], axis=1))
    side = rq[0, :, 256:384]
    for i in range(1, 8):
        side = side + rq[i, :, 256:384]
    gside_ref[...] = mine(side)
    gproj_ref[...] = mine(jnp.concatenate([rp[i] for i in range(8)], axis=1))

    for i in range(2):
        done = finish(a[i][1])
        gin_ref[i] = done[0:32]
        gout_ref[i] = done[32:48]
    for i in range(2):
        for rings in (a, b, dn):
            rings[i][0].sent()
            rings[i][1].sent()
    each_piece(lambda c: c.wait_send(), False)


def call(kernel, outs, scratch, args, name, collective=None, **more):
    params = dict(vmem_limit_bytes=VMEM_LIMIT)
    if collective is not None:
        params.update(collective_id=collective, has_side_effects=True)
    space = pl.BlockSpec(memory_space=pltpu.VMEM)
    return pl.pallas_call(
        kernel,
        out_shape=[jax.ShapeDtypeStruct(shape, kind) for shape, kind in outs],
        in_specs=more.pop("in_specs", [space] * len(args)),
        out_specs=more.pop("out_specs", [space] * len(outs)),
        scratch_shapes=scratch,
        compiler_params=pltpu.CompilerParams(**params),
        name=name,
        **more,
    )(*args)


def sems(*sizes):
    return [pltpu.SemaphoreType.DMA(s if isinstance(s, tuple) else (s,)) for s in sizes]


def body(
    layer_input, gain_attn, w_query, w_key, w_value, w_proj, gain_ffn, w_router,
    w_expert_in, w_expert_out, segment_ids, expert_ids, slot_order, out_grad,
):
    ep = lax.axis_index("ep")
    gain_one, gain_two = gain_attn.reshape(1, 1024), gain_ffn.reshape(1, 1024)
    tables = [jnp.asarray(t) for t in rope_tables()]
    w_own = jnp.concatenate(
        [
            lax.dynamic_slice_in_dim(w_query, ep * 128, 128, 1),
            lax.dynamic_slice_in_dim(w_key, ep * 64, 64, 1),
            lax.dynamic_slice_in_dim(w_value, ep * 64, 64, 1),
        ],
        axis=1,
    )
    wr_rows = jnp.pad(w_router.T.reshape(8, 4, 1024), ((0, 0), (0, 4), (0, 0))).reshape(64, 1024)
    w_proj_own = lax.dynamic_slice_in_dim(w_proj, ep * 128, 128, 0)
    order = slot_order.reshape(TOK, 8)
    docs = segment_ids.reshape(32, 128)

    normed_all, query, kv, grad_all, slots, chosen, starts = call(
        first_kernel,
        [
            ((8, TOK, 1024), BF16), ((8, TOK, 128), BF16), ((8, 4, TOK, 128), BF16), ((8, TOK, 1024), BF16),
            ((8, 8, TOK), F32), ((64, TOK), F32), ((32, 128), F32),
        ],
        [pltpu.VMEM((8, 8, TOK), F32)] + sems(13, 13, 13, 13, 8, 8, 24, 24),
        [layer_input, gain_one, out_grad, w_own, *tables, expert_ids, expert_ids.T, order, order.T, docs],
        "first", 1,
    )
    kv_rows = kv.reshape(4096, 128)
    ctx = lax.axis_index("ctx")
    first = lax.dynamic_slice_in_dim(starts.reshape(8, 4, 128), ctx, 1, 1)[:, 0, 0].astype(jnp.int32) // CHUNK

    vm, sm = pl.BlockSpec(memory_space=pltpu.VMEM), pl.BlockSpec(memory_space=pltpu.SMEM)
    attended, attended_tall, log_sums = call(
        attend_kernel,
        [((8, TOK, 128), BF16), ((8, 128, TOK), F32), ((8, 8, 256), F32)],
        [pltpu.VMEM((128, 4096), BF16)],
        [first, query, kv_rows, starts],
        "attend", in_specs=[sm, vm, vm, vm],
    )
    residual, ffn_all, gates_in, gates = call(
        middle_kernel,
        [((TOK, 1024), F32), ((8, TOK, 1024), BF16), ((8, 8, TOK), F32), ((64, TOK), F32)],
        [pltpu.VMEM((8, TOK, 128), BF16), pltpu.VMEM((8, 8, TOK), F32)] + sems(8, 8, 13, 13, 8, 8),
        [attended, layer_input, gain_two, w_proj, wr_rows, chosen],
        "middle", 2,
    )
    whole = lambda *shape: pl.BlockSpec(shape, lambda j: (0,) * len(shape))
    sums, back, grad_gates, grad_experts = call(
        expert_kernel,
        [((8, TOK, 1024), BF16), ((8, TOK, 1024), BF16), ((8, 8, TOK), F32), ((4, 32, 48, 1024), BF16)],
        [pltpu.VMEM((4, 8 * CAP, 1024), F32), pltpu.VMEM((4, 8 * CAP, 1024), F32)],
        [ffn_all, grad_all, slots, gates_in, w_expert_in, w_expert_out],
        "experts", grid=(4,),
        in_specs=[
            whole(8, TOK, 1024), whole(8, TOK, 1024), whole(8, 8, TOK), whole(8, 8, TOK),
            pl.BlockSpec((1, 1024, 1024), lambda j: (j, 0, 0)), pl.BlockSpec((1, 512, 1024), lambda j: (j, 0, 0)),
        ],
        out_specs=[
            whole(8, TOK, 1024), whole(8, TOK, 1024), whole(8, 8, TOK),
            pl.BlockSpec((1, 32, 48, 1024), lambda j: (j, 0, 0, 0)),
        ],
    )
    own_ffn = lax.dynamic_index_in_dim(ffn_all, ep, 0, False)
    grad_mixed, grad_res, grad_router, grad_gain_two = call(
        turn_kernel,
        [((8, TOK, 1024), BF16), ((TOK, 1024), F32), ((64, 1024), F32), ((8, 1024), F32)],
        [pltpu.VMEM((8, 8, TOK), F32)] + scatter_sum_scratch() + sems(8, 8, 13, 13),
        [back, grad_gates, gates, residual, own_ffn, out_grad, gain_two, wr_rows],
        "turn", 3,
    )
    grad_q, grad_kv, grad_proj = call(
        attend_back_kernel,
        [((8, TOK, 128), BF16), ((4096, 128), BF16), ((128, 1024), F32)],
        [pltpu.VMEM((HD, 4096), BF16), pltpu.VMEM((4096, 128), F32)],
        [first, query, kv_rows, starts, attended_tall, log_sums, grad_mixed, w_proj_own, *tables],
        "attend_back", in_specs=[sm] + [vm] * 11,
    )
    layer_output, input_grad, dense = call(
        final_kernel,
        [((TOK, 1024), BF16), ((TOK, 1024), BF16), ((32, 32, 512), BF16)],
        [pltpu.VMEM((2, 4, 8, TOK, 128), BF16), pltpu.VMEM((8, TOK, 256), BF16), pltpu.VMEM((8, TOK, 256), BF16)]
        + scatter_sum_scratch() + sems(16, 16, 8, 8),
        [
            grad_q, grad_kv.reshape(8, 4, TOK, 128), sums, residual, layer_input, gain_one, normed_all,
            w_query, w_key, w_value, grad_res, *tables, grad_router, grad_gain_two, grad_proj,
        ],
        "final", 4,
    )
    grad_in, grad_out, out_q, out_k, out_v, side, out_proj = call(
        sums_kernel,
        [
            ((4, 32, 1024), F32), ((4, 16, 1024), F32), ((4, 1024), F32), ((4, 512), F32), ((4, 512), F32),
            ((4, 128), F32), ((4, 1024), F32),
        ],
        [
            pltpu.VMEM((2, 3, 2, 4, 48, 1024), BF16), pltpu.VMEM((2, 7, 48, 1024), BF16),
            pltpu.VMEM((2, 7, 4, 48, 1024), BF16), pltpu.VMEM((2, 3, 48, 1024), BF16),
            pltpu.VMEM((2, 3, 2, 4, 16, 512), BF16), pltpu.VMEM((2, 7, 16, 512), BF16),
            pltpu.VMEM((2, 2, 4, 48, 1024), BF16), pltpu.VMEM((2, 4, 48, 1024), BF16),
            pltpu.VMEM((2, 2, 4, 16, 512), BF16),
            pltpu.VMEM((4, 8, 512), F32), pltpu.VMEM((8, 8, 384), F32), pltpu.VMEM((8, 8, 128), F32),
        ]
        + sems((2, 3), (2, 3), (2, 7), (2, 7), (2, 7), (2, 7), (2, 3), (2, 3), (2, 3), (2, 3), (2, 7), (2, 7), 8, 8, 8, 8),
        [grad_experts.reshape(4, 2, 4, 4, 48, 1024), dense.reshape(2, 4, 4, 32, 512)],
        "sums", 5,
    )
    router = side[:, :64].reshape(4, 8, 8)[:, :, :4].reshape(4, 32)
    return (
        layer_output, input_grad, side[:, 64], out_q, out_k, out_v, out_proj, side[:, 72], router, grad_in, grad_out,
    )


def solution(mesh):
    tokens = P(("dp", "ep", "ctx"), None)
    in_specs = (
        tokens, P(), P(), P(), P(), P(), P(), P(),
        P("ep", None, None), P("ep", None, None), P("dp", None), tokens, tokens, tokens,
    )
    out_specs = (
        tokens, tokens, P(("dp", "ep", "ctx")), tokens, tokens, tokens, tokens, P(("dp", "ep", "ctx")), tokens,
        P("ep", ("dp", "ctx"), None), P("ep", ("dp", "ctx"), None),
    )
    return jax.shard_map(body, mesh=mesh, in_specs=in_specs, out_specs=out_specs, check_vma=False)
```

time: 1580 us -> 373 us (0.24)
  waiting for transfers between devices: 1040 us -> 0 us
  Pallas kernels: 0 us -> 346 us
  matrix products: 196 us -> 0 us
  blocking collectives: 159 us -> 0 us
  local copies, waits for them, and re-layouts: 98.5 us -> 21.2 us
  other arithmetic: 48.5 us -> 2.14 us
    unnamed x10 -> x0, waiting for transfers between devices: 560 us -> none
    pallas_call x0 -> x8, Pallas kernels: none -> 346 us  [call(): pl.pallas_call(kernel, out_shape=[jax.ShapeDtypeStruct(shape, kind) for s...]
    reduce_scatter x2 -> x0, waiting for transfers between devices: 269 us -> none  [the longest x1 164 us: body(): lax.psum_scatter(grad_w_out.astype(jnp.bfloat16), ('dp', 'ctx'), scatter_...]
    dot_general x81 -> x0, matrix products: 196 us -> none  [the longest x8 22.4 us: backward_group(): jnp.einsum('gqd,kd->gqk', query_grp, key_head, preferred_element_type=jnp...]
    all_gather x2 -> x0, waiting for transfers between devices: 162 us -> none  [the longest x1 82.7 us: fetch_keys(): lax.all_gather(key_rot, ('ep', 'ctx'), axis=0, tiled=True)]
    all_to_all x2 -> x0, blocking collectives: 82.9 us -> none  [the longest x1 47.3 us: body(): lax.all_to_all(outgoing, 'ep', split_axis=1, concat_axis=1, tiled=True)]
    unnamed x1 -> x0, blocking collectives: 76.1 us -> none
    all_to_all x2 -> x0, waiting for transfers between devices: 50.4 us -> none  [the longest x1 25.8 us: body(): lax.all_to_all(expert_out.reshape(local_experts, ep_count, capacity, -1),...]
  transfers between devices with their start and end apart: 9 -> 0, of which waited for: 9 -> 0; matrix products, arithmetic and copies ran while one was open for 5% -> 0% of each run, Pallas kernels for 0% -> 0%
where the time goes in v1:
time: 373 us; the launch traced here: 370 us
  Pallas kernels  346 us (93%)
  local copies, waits for them, and re-layouts  21.2 us (6%)
    pallas_call x8, Pallas kernels, call(): pl.pallas_call(kernel, out_shape=[jax.ShapeDtypeStruct(shape, kind) for s...  346 us
    unnamed x25, local copies, waits for them, and re-layouts  10.6 us

profile of v1, /device:TPU:8, one launch (start us, length us, event | category | flops | bytes accessed | tf_op | source)
XLA Modules:
  0.0 370.4 jit_solution(4991179722520566275)
XLA Ops:
  0.6 0.0 copy-start.5
  0.7 0.0 copy-start.6
  0.7 1.2 constant_dynamic-slice_fusion.2
  1.9 1.0 constant_dynamic-slice_fusion.4
  2.9 0.0 copy-start.4
  2.9 1.0 pad_maximum_fusion.w_ref
  3.9 0.0 copy-done.5
  3.9 0.7 copy.33.eid_ref
  4.6 0.5 broadcast.20
  5.1 0.0 copy-done.6
  5.1 0.7 reduce.7
  5.8 0.1 reshape.63.so_ref
  5.9 0.0 copy-start
  5.9 0.7 copy.32
  6.5 0.0 copy-done
  6.6 37.2 %first.1 = (bf16[8,128,1024]{2,1,0:T(8,128)(2,1)}, bf16[8,128,128]{2,1,0:T(8,128)(2,1)}, bf16[8,4,128,128]{3,2,1,0:T(8,128)(2,1)}, bf16[8,128,1024]{2,1,0:T(8,12...) custom-call(bf16[128,1024]{1,0:T(8,128)(2,1)} %x_ref.5, f32[1,1024]{1,0:T(1,128)} %bitcast.37, ...), custom_call_target="tpu_custom_call" | custom-call | tf_op jit(solution)/shard_map/first/pallas_call | solution.py:1054
  43.8 0.7 constant_dynamic-slice_fusion.1
  44.5 0.1 copy.36
  44.6 0.5 and_select_fusion.first_ref
  45.1 19.0 %attend.1 = (bf16[8,128,128]{2,1,0:T(8,128)(2,1)}, f32[8,128,128]{2,1,0:T(8,128)}, f32[8,8,256]{2,1,0:T(8,128)}) custom-call(s32[8]{0:T(128)} %and_select_fusion.first_ref, bf16[8,128,128]{2,1,0:T(8,128)(2,1)} %get-tuple-element.47.q_ref, bf16[4096,128]{1,0:T(8,128)(2,1)} %bitcast.26, f32[32,128]{1,0:T(8,128)} %get-tuple-element.46.start_ref), custom_call_target="tpu_custom_call" | custom-call | tf_op jit(solution)/shard_map/attend/pallas_call | solution.py:1054
  64.1 0.0 copy-done.4
  64.1 0.7 pad_bitcast_fusion.wr_ref
  64.8 25.6 %middle.1 = (f32[128,1024]{1,0:T(8,128)}, bf16[8,128,1024]{2,1,0:T(8,128)(2,1)}, f32[8,8,128]{2,1,0:T(8,128)}, f32[64,128]{1,0:T(8,128)}) custom-call(bf16[8,128,128]{2,1,0:T(8,128)(2,1)} %get-tuple-element.51.att_ref, bf16[128,1024]{1,0:T(8,128)(2,1)} %x_ref.5, f32[1,1024]{1,0:T(1,128)} %bitcast.35, bf16[1024,1024]{1,0:T(8,128)(2,1)} %w_ref.1, ...), custom_call_target="tpu_custom_call" | custom-call | tf_op jit(solution)/shard_map/middle/pallas_call | solution.py:1054
  90.5 28.6 %experts.1 = (bf16[8,128,1024]{2,1,0:T(8,128)(2,1)}, bf16[8,128,1024]{2,1,0:T(8,128)(2,1)}, f32[8,8,128]{2,1,0:T(8,128)}, bf16[4,32,48,1024]{3,2,1,0:T(8,128)(2,1)}) custom-call(bf16[8,128,1024]{2,1,0:T(8,128)(2,1)} %get-tuple-element.53.nf_ref, bf16[8,128,1024]{2,1,0:T(8,128)(2,1)} %get-tuple-element.54.og_ref, f32[8,8,128]{2,1,0:T(8,128)} %get-tuple-element.55.slot_ref, ...), custom_call_target="tpu_custom_call" | custom-call | tf_op jit(solution)/shard_map/experts/pallas_call | solution.py:1054
  119.1 1.7 dynamic-slice_bitcast_fusion.nf_ref
  120.8 32.7 %turn.1 = (bf16[8,128,1024]{2,1,0:T(8,128)(2,1)}, f32[128,1024]{1,0:T(8,128)}, f32[64,1024]{1,0:T(8,128)}, f32[8,1024]{1,0:T(8,128)}) custom-call(bf16[8,128,1024]{2,1,0:T(8,128)(2,1)} %get-tuple-element.57.part_ref, f32[8,8,128]{2,1,0:T(8,128)} %get-tuple-element.58.dg_ref, f32[64,128]{1,0:T(8,128)} %get-tuple-element.59.gates_ref, ...), custom_call_target="tpu_custom_call" | custom-call | tf_op jit(solution)/shard_map/turn/pallas_call | solution.py:1054
  153.5 1.7 constant_dynamic-slice_fusion.w_ref
  155.1 22.7 %attend_back.1 = (bf16[8,128,128]{2,1,0:T(8,128)(2,1)}, bf16[4096,128]{1,0:T(8,128)(2,1)}, f32[128,1024]{1,0:T(8,128)}) custom-call(s32[8]{0:T(128)} %and_select_fusion.first_ref, bf16[8,128,128]{2,1,0:T(8,128)(2,1)} %get-tuple-element.47.q_ref, bf16[4096,128]{1,0:T(8,128)(2,1)} %bitcast.27, f32[32,128]{1,0:T(8,128)} %get-tuple-element.46.start_ref, ...), custom_call_target="tpu_custom_call" | custom-call | tf_op jit(solution)/shard_map/attend_back/pallas_call | solution.py:1054
  177.8 41.1 %final.1 = (bf16[128,1024]{1,0:T(8,128)(2,1)}, bf16[128,1024]{1,0:T(8,128)(2,1)}, bf16[32,32,512]{2,1,0:T(8,128)(2,1)}) custom-call(bf16[8,128,128]{2,1,0:T(8,128)(2,1)} %get-tuple-element.62.dq_ref, bf16[8,4,128,128]{3,2,1,0:T(8,128)(2,1)} %bitcast.28, bf16[8,128,1024]{2,1,0:T(8,128)(2,1)} %get-tuple-element.64.part_ref, ...), custom_call_target="tpu_custom_call" | custom-call | tf_op jit(solution)/shard_map/final/pallas_call | solution.py:1054
  218.9 0.0 copy-start.2
  218.9 0.0 copy-start.1
  218.9 139.4 %sums.1 = (f32[4,32,1024]{2,1,0:T(8,128)}, f32[4,16,1024]{2,1,0:T(8,128)}, f32[4,1024]{1,0:T(4,128)}, f32[4,512]{1,0:T(4,128)}, f32[4,512]{1,0:T(4,128)}, /*index=5*/f32[4,128]{1,0:T(4,128)}, f32[4,1024]{1,0:T(4,128)}) custom-call(bf16[4,2,4,4,48,1024]{5,4,3,2,1,0:T(8,128)(2,1)} %bitcast.25, bf16[2,4,4,32,512]{4,3,2,1,0:T(8,128)(2,1)} %bitcast.29), custom_call_target="tpu_custom_call" | custom-call | tf_op jit(solution)/shard_map/sums/pallas_call | solution.py:1054
  358.3 0.0 copy-start.3
  358.3 1.5 slice_reduce_fusion
  359.8 0.7 reshape.73
  360.5 0.7 reshape.74
  361.2 0.0 copy-done.2
  361.2 0.7 copy.45
  361.9 0.0 copy-done.1
  361.9 0.7 copy.46
  362.6 1.3 copy.47
  363.9 1.3 copy.48
  365.2 1.3 copy.49
  366.5 1.3 copy.50
  367.9 1.9 copy.51
  369.7 0.0 copy-done.3
  369.7 0.7 copy.52
  (1 shorter events, 0.0 us)
Async XLA Ops:
  0.6 3.2 copy-start.5
  0.7 4.5 %copy-start.6 = (s32[1,1024]{1,0:T(1,128)S(1)}, s32[1,1024]{1,0:T(1,128)}, u32[]{:S(2)}) copy-start(s32[1,1024]{1,0:T(1,128)} %param.30) | copy-start | bytes 12292
  2.9 61.2 %copy-start.4 = (bf16[1024,32]{0,1:T(8,128)(2,1)S(1)}, bf16[1024,32]{0,1:T(8,128)(2,1)}, u32[]{:S(2)}) copy-start(bf16[1024,32]{0,1:T(8,128)(2,1)} %param.25) | copy-start | bytes 196612
  5.9 0.7 copy-start
  218.9 142.3 %copy-start.2 = (bf16[128,1024]{1,0:T(8,128)(2,1)S(1)}, bf16[128,1024]{1,0:T(8,128)(2,1)}, u32[]{:S(2)}) copy-start(bf16[128,1024]{1,0:T(8,128)(2,1)} %get-tuple-element.96) | copy-start | bytes 786436
  218.9 143.0 %copy-start.1 = (bf16[128,1024]{1,0:T(8,128)(2,1)S(1)}, bf16[128,1024]{1,0:T(8,128)(2,1)}, u32[]{:S(2)}) copy-start(bf16[128,1024]{1,0:T(8,128)(2,1)} %get-tuple-element.97) | copy-start | bytes 786436
  358.3 11.4 %copy-start.3 = (f32[4,16,1024]{2,1,0:T(8,128)S(1)}, f32[4,16,1024]{2,1,0:T(8,128)}, u32[]{:S(2)}) copy-start(f32[4,16,1024]{2,1,0:T(8,128)} %get-tuple-element.106) | copy-start | bytes 786436

commit v2 on v1

--- a/solution.py
+++ b/solution.py
@@ -594,12 +594,14 @@
         dg_ref[s, pl.ds(j, 1), :] = jnp.sum(
             jnp.where(picks(s, j), dots[s * CAP : (s + 1) * CAP], 0.0), axis=0, keepdims=True
         )
-    gw_ref[0, :, 32:48, :] = mm(act, grad_res, TN).astype(BF16).reshape(32, 16, 1024)
+    gw_ref[2] = mm(act, grad_res, TN).astype(BF16).reshape(32, 16, 1024)
     grad_act = mm(grad_res, wout_ref[0], NT)
     grad_up = (grad_act * silu).astype(BF16)
     grad_gate = (grad_act * up * sig * (1.0 + gating * (1.0 - sig))).astype(BF16)
     grad_gu = jnp.concatenate([grad_gate, grad_up], axis=1)
-    gw_ref[0, :, 0:32, :] = mm(received, grad_gu, TN).astype(BF16).reshape(32, 32, 1024)
+    grad_in = mm(received, grad_gu, TN).astype(BF16).reshape(32, 32, 1024)
+    gw_ref[0] = grad_in[:, 0:16]
+    gw_ref[1] = grad_in[:, 16:32]
     rows_scr[j] = mm(grad_gu, win_ref[0], NT)
 
     @pl.when(j == 3)
@@ -617,72 +619,347 @@
         lax.fori_loop(0, 8, store, 0)
 
 
+def each_slab(lead, work):
+    count = 1
+    for size in lead:
+        count *= size
+
+    def each(i, carry):
+        work((i,) if len(lead) == 1 else (i // lead[1], i % lead[1]))
+        return carry
+
+    lax.fori_loop(0, count, each, 0)
+
+
+class Arc:
+    def __init__(self, n, pos, own, half, slots, devices, send, recv):
+        self.n, self.pos, self.own, self.half, self.slots = n, pos, own, half, slots
+        self.devices, self.send, self.recv = devices, send, recv
+        self.steps = n // 2
+
+    def chunk(self, way, s):
+        reach = self.steps - s + 1
+        return (self.pos + reach) % self.n if way == 0 else (self.pos + self.n - reach) % self.n
+
+    def copy(self, way, s):
+        dst = self.slots.at[way, s - 1]
+        src = self.own(self.chunk(way, s)) if s == 1 else self.slots.at[way, s - 2]
+        if s == 1:
+            src, dst = self.half(src, way), self.half(dst, way)
+        return remote(src, dst, self.send.at[way, s - 1], self.recv.at[way, s - 1], self.devices[way])
+
+    def start(self):
+        for way in (0, 1):
+            self.copy(way, 1).start()
+
+    def slabs(self, work):
+        each_slab(self.slots.shape[2:-2], work)
+
+    def advance(self, s):
+        for way in (0, 1):
+            self.copy(way, s - 1).wait_recv()
+            held, own = self.slots.at[way, s - 2], self.own(self.chunk(way, s))
+            if s == 2:
+                self.merge(way, held, own)
+            else:
+
+                def add(index):
+                    held[index] = (held[index].astype(F32) + own[index].astype(F32)).astype(BF16)
+
+                self.slabs(add)
+            self.copy(way, s).start()
+
+    def merge(self, way, held, own):
+        mine, its = self.half(held, way), self.half(own, way)
+        other, from_own = self.half(held, 1 - way), self.half(own, 1 - way)
+
+        def add(index):
+            mine[index] = (mine[index].astype(F32) + its[index].astype(F32)).astype(BF16)
+
+        def take(index):
+            other[index] = from_own[index]
+
+        each_slab(mine.shape[:-2], add)
+        each_slab(other.shape[:-2], take)
+
+    def finish(self, put):
+        for way in (0, 1):
+            self.copy(way, self.steps).wait_recv()
+        own, up, down = self.own(self.pos), self.slots.at[0, self.steps - 1], self.slots.at[1, self.steps - 1]
+
+        def add(index):
+            put(index, own[index].astype(F32) + up[index].astype(F32) + down[index].astype(F32))
+
+        self.slabs(add)
+
+    def sent(self):
+        for way in (0, 1):
+            for s in range(1, self.steps + 1):
+                self.copy(way, s).wait_send()
+
+
+class Torus:
+    def __init__(self, place):
+        self.dp, self.ep, self.ctx = place
+        self.zh, self.x = self.dp // 4, self.dp % 4
+        self.z = self.zh * 4 + self.ctx
+
+    def at_x(self, v):
+        return (self.zh * 4 + v % 4, self.ep, self.ctx)
+
+    def at_z(self, v):
+        v = v % 8
+        return ((v // 4) * 4 + self.x, self.ep, v % 4)
+
+    def x_ways(self):
+        return self.at_x(self.x + 1), self.at_x(self.x + 3)
+
+    def z_ways(self):
+        return self.at_z(self.z + 1), self.at_z(self.z + 7)
+
+    def x_arc(self, own, half, slots, send, recv):
+        return Arc(4, self.x, own, half, slots, self.x_ways(), send, recv)
+
+    def z_arc(self, own, half, slots, send, recv):
+        return Arc(8, self.z, own, half, slots, self.z_ways(), send, recv)
+
+
+def first_or_last(sizes):
+    def half(view, h):
+        return view.at[pl.ds(0, sizes[0])] if h == 0 else view.at[pl.ds(sizes[0], sizes[1])]
+
+    return half
+
+
+X_TURN, Z_TURN, X_FINAL, Z_FINAL = (0, 1, 2, 3), (9, 10, 11), (4, 5, 6, 7), (8,)
+
+
+def unit_arcs(torus, own, x_units, z_units, x_slots, z_slots, xs, xr, zs, zr):
+    xa = [
+        torus.x_arc(
+            lambda t, i=i: own.at[i, :, t], first_or_last((1, 1)), x_slots.at[i], xs.at[i], xr.at[i]
+        )
+        for i in range(len(x_units))
+    ]
+    za = [
+        torus.z_arc(
+            lambda t, i=i: own.at[len(x_units) + i, t // 4, :, t % 4], first_or_last((2, 2)), z_slots.at[i], zs.at[i], zr.at[i]
+        )
+        for i in range(len(z_units))
+    ]
+    return xa, za
+
+
+def fetch_units(gw_ref, own, sem, units):
+    return [pltpu.make_async_copy(gw_ref.at[u], own.at[i], sem.at[i]) for i, u in enumerate(units)]
+
+
 def turn_kernel(
-    part_ref, dg_ref, gates_ref, res_ref, nf_ref, og_ref, gain_ref, wr_ref,
-    gm_ref, gres_ref, grouter_ref, ggain_ref,
+    part_ref, dg_ref, gates_ref, res_ref, nf_ref, og_ref, gain_ref, wr_ref, gw_ref,
+    gm_ref, gres_ref, grouter_ref, ggain_ref, rx_ref, rz_ref,
     dbuf, cbuf, fbuf, gbuf, csend, crecv, dsend, drecv, gsend, grecv,
+    own, x_slots, z_slots, usem, xs, xr, zs, zr,
 ):
     place = where_am_i()
     dp, ep, ctx = place
+    torus = Torus(place)
+    fetches = fetch_units(gw_ref, own, usem, X_TURN + Z_TURN)
+    for f in fetches:
+        f.start()
     barrier = pltpu.get_barrier_semaphore()
     for r in range(1, 8):
         greet(barrier, (dp, (ep + r) % 8, ctx))
-    pl.semaphore_wait(barrier, 7)
+    for device in torus.x_ways() + torus.z_ways():
+        greet(barrier, device)
+    pl.semaphore_wait(barrier, 11)
     total = EpScatterSum(part_ref, cbuf, fbuf, gbuf, csend, crecv, place)
     total.start()
     exchange(dg_ref, dbuf, dsend, drecv, place, False)
     dbuf[ep] = dg_ref[ep]
+    xa, za = unit_arcs(torus, own, X_TURN, Z_TURN, x_slots, z_slots, xs, xr, zs, zr)
+    for i in range(4):
+        fetches[i].wait()
+        xa[i].start()
+        if i < 3:
+            fetches[4 + i].wait()
+            za[i].start()
     total.far()
+    za[0].advance(2)
+    xa[0].advance(2)
+    za[1].advance(2)
     total.near()
+    xa[1].advance(2)
+    za[2].advance(2)
     exchange(dg_ref, dbuf, dsend, drecv, place, True)
     gates = gates_ref[...]
     grad_gates = jnp.concatenate([dbuf[p] for p in range(8)], axis=0)
     grad_logits = gates * (grad_gates - jnp.sum(gates * grad_gates, axis=0, keepdims=True))
     high = grad_logits.astype(BF16)
     low = (grad_logits - high.astype(F32)).astype(BF16)
-    grouter_ref[...] = mm(high, nf_ref[...]) + mm(low, nf_ref[...])
+    to = lax.broadcasted_iota(jnp.int32, (32, 64), 0)
+    source = lax.broadcasted_iota(jnp.int32, (32, 64), 1)
+    squeeze = jnp.where(source == (to // 4) * 8 + to % 4, 1.0, 0.0).astype(BF16)
+    grouter_ref[...] = mm(mm(squeeze, high).astype(BF16), nf_ref[...]) + mm(mm(squeeze, low).astype(BF16), nf_ref[...])
     from_router = mm(high, wr_ref[...], TN) + mm(low, wr_ref[...], TN)
     res = res_ref[...]
     scale = lax.rsqrt(jnp.mean(res * res, axis=-1, keepdims=True) + EPSILON)
+    scaled = res * scale
+    za[0].advance(3)
+    xa[2].advance(2)
+    za[1].advance(3)
     grad_normed = total.last() + from_router
-    scaled = res * scale
     ggain_ref[...] = jnp.broadcast_to(jnp.sum(grad_normed * scaled, axis=0, keepdims=True), (8, 1024))
     grad_normed = grad_normed * gain_ref[...]
     mean = jnp.mean(grad_normed * scaled, axis=-1, keepdims=True)
     gres = og_ref[...].astype(F32) + scale * (grad_normed - scaled * mean)
-    gres_ref[...] = gres
     gm_ref[ep] = gres.astype(BF16)
     gather = EpGather(gm_ref, gsend, grecv, place)
     gather.go(0, 1, 3, 2, 4)
-    gather.whole()
+    gres_ref[...] = gres
+    xa[3].advance(2)
+    za[2].advance(3)
+    gather.got(1)
+    gather.go(5, 6)
+    gather.got(3)
+    gather.go(7, 8)
+    za[0].advance(4)
+    gather.got(2)
+    gather.go(9)
+    gather.got(4)
+    gather.go(10)
+    za[1].advance(4)
+    gather.got(5)
+    gather.go(11)
+    gather.got(7)
+    gather.go(12)
+    za[2].advance(4)
+    gather.got(0, 6, 8, 9, 10, 11, 12)
+
+    for i in range(4):
+
+        def put_x(index, value, i=i):
+            rx_ref[index[0] * 4 + index[1], i] = value.astype(BF16)
+
+        xa[i].finish(put_x)
+        if i < 3:
+
+            def put_z(index, value, i=i):
+                rz_ref[index[0], i] = value.astype(BF16)
+
+            za[i].finish(put_z)
     gather.sent()
     exchange_sent(dg_ref, dbuf, dsend, drecv, place)
     total.sent()
+    for arc in xa + za:
+        arc.sent()
+
+
+class Direct:
+    def __init__(self, torus, part, x_slots, result, z_slots, send, recv):
+        self.t, self.part, self.x_slots, self.result, self.z_slots = torus, part, x_slots, result, z_slots
+        self.send, self.recv = send, recv
+
+    def x_copy(self, r):
+        to = (self.t.x + r) % 4
+        return remote(
+            self.part.at[:, to], self.x_slots.at[r - 1], self.send.at[r], self.recv.at[r], self.t.at_x(to)
+        )
+
+    def z_copy(self, r):
+        to = (self.t.z + r) % 8
+        return remote(
+            self.result.at[to], self.z_slots.at[r - 1], self.send.at[3 + r], self.recv.at[3 + r], self.t.at_z(to)
+        )
+
+    def start(self):
+        for r in (2, 1, 3):
+            self.x_copy(r).start()
+
+    def turn(self):
+        for r in (1, 2, 3):
+            self.x_copy(r).wait_recv()
+
+        def add(i, carry):
+            h, l = i // 4, i % 4
+            value = self.part[h, self.t.x, l].astype(F32)
+            for r in range(3):
+                value = value + self.x_slots[r, h, l].astype(F32)
+            self.result[i] = value.astype(BF16)
+            return carry
+
+        lax.fori_loop(0, 8, add, 0)
+        for r in (4, 3, 5, 2, 6, 1, 7):
+            self.z_copy(r).start()
+
+    def finish(self):
+        for r in range(1, 8):
+            self.z_copy(r).wait_recv()
+        value = self.result[self.t.z].astype(F32)
+        for r in range(7):
+            value = value + self.z_slots[r].astype(F32)
+        return value
+
+    def sent(self):
+        for r in (1, 2, 3):
+            self.x_copy(r).wait_send()
+        for r in range(1, 8):
+            self.z_copy(r).wait_send()
 
 
 def final_kernel(
-    dq_ref, dkv_ref, part_ref, res_ref, x_ref, gain_ref, nall_ref, wq_ref, wk_ref, wv_ref, gres_ref,
-    ca_ref, sa_ref, cb_ref, sb_ref, grouter_ref, ggain_ref, gproj_ref,
-    out_ref, ing_ref, dense_ref,
-    kbuf, dqkv, pieces, cbuf, fbuf, gbuf, csend, crecv, ksend, krecv, psend, precv,
+    dq_ref, dkv_ref, x_ref, gain_ref, ca_ref, sa_ref, cb_ref, sb_ref, grouter_ref, ggain_ref, gproj_ref, rx_ref, rz_ref,
+    part_hbm, res_hbm, nall_hbm, wq_hbm, wk_hbm, wv_hbm, gres_hbm, gw_ref,
+    out_ref, ing_ref, gin_ref, gout_ref, gq_ref, gk_ref, gv_ref, gside_ref, gproj_out, gains_ref,
+    part, res, nall, wq, wk, wv, gres,
+    kbuf, dkvb, qpieces, kpieces, cbuf, fbuf, gbuf,
+    own, x_slots, z_slots, g0_slots, g1_slots, h0_slots, h1_slots, rx1, rz1,
+    early, late, e_x, e_res, e_z, l_x, l_res, l_z, gain_own, gain_e, gain_x, gain_z, fin, rq, rp,
+    fsem, csend, crecv, ksend, krecv, qsend, qrecv, psend, precv, usem, xs, xr, zs, zr,
+    g0s, g0r, g1s, g1r, h0s, h0r, h1s, h1r, es, er, ls, lr, gs, gr, fsend, frecv, hsend, hrecv,
 ):
     place = where_am_i()
     dp, ep, ctx = place
+    torus = Torus(place)
+    loads = [
+        pltpu.make_async_copy(src, dst, fsem.at[i])
+        for i, (src, dst) in enumerate(
+            ((part_hbm, part), (nall_hbm, nall), (wq_hbm, wq), (wk_hbm, wk), (wv_hbm, wv), (res_hbm, res), (gres_hbm, gres))
+        )
+    ]
+    fetches = fetch_units(gw_ref, own, usem, X_FINAL + Z_FINAL)
+    loads[0].start()
+    for f in fetches:
+        f.start()
+    for f in loads[1:]:
+        f.start()
+
+    def send_to(g, h):
+        return (dp, 2 * ctx + g // 2, 2 * (g % 2) + h), (ep, 2 * ctx + g // 2, 2 * (g % 2) + h)
+
+    def is_me(device):
+        return (device[0] == dp) & (device[1] == ep) & (device[2] == ctx)
+
     barrier = pltpu.get_barrier_semaphore()
     for r in range(1, 8):
         greet(barrier, (dp, (ep + r) % 8, ctx))
-
-    @pl.when(ctx > 0)
-    def _():
-        greet(barrier, (dp, ep, ctx - 1))
-
-    @pl.when(ctx < 3)
-    def _():
-        greet(barrier, (dp, ep, ctx + 1))
-
-    edges = jnp.where(ctx > 0, 1, 0) + jnp.where(ctx < 3, 1, 0)
-    pl.semaphore_wait(barrier, 7 + edges)
-    total = EpScatterSum(part_ref, cbuf, fbuf, gbuf, csend, crecv, place)
+        greet(barrier, torus.at_z(torus.z + r))
+    for r in range(1, 4):
+        greet(barrier, torus.at_x(torus.x + r))
+    for i in range(8):
+        for device in ((dp, i, ep // 2), (i, dp, ep // 2)):
+
+            @pl.when(jnp.logical_not(is_me(device)))
+            def _():
+                greet(barrier, device)
+
+    waits = 17
+    for g in range(4):
+        for h in range(2):
+            for device in send_to(g, h):
+                waits = waits + jnp.where(is_me(device), 0, 1)
+    pl.semaphore_wait(barrier, waits)
+
+    total = EpScatterSum(part, cbuf, fbuf, gbuf, csend, crecv, place)
 
     def link(direction, shard, half, action):
         blocks = pl.ds(half * 4, 4)
@@ -695,7 +972,7 @@
         else:
             passes, middle, here = ctx > shard, (ctx > shard) & (ctx < 3), (ctx == shard) & (ctx < 3)
         slot = kbuf.at[direction, shard, blocks]
-        own = dkv_ref.at[blocks, shard]
+        mine = dkv_ref.at[blocks, shard]
 
         def copy(src):
             return remote(src, slot, send, recv, (dp, ep, to))
@@ -704,7 +981,7 @@
 
             @pl.when(passes & first)
             def _():
-                copy(own).start()
+                copy(mine).start()
 
             @pl.when(middle)
             def _():
@@ -732,18 +1009,60 @@
             def _():
                 copy(slot).wait_send()
 
-    for half in (0, 1):
-        link(0, 3, half, "send")
-        link(1, 0, half, "send")
+    def links(right, left, action):
+        for half in (0, 1):
+            link(0, right, half, action)
+            link(1, left, half, action)
+
+    xa, za = unit_arcs(torus, own, X_FINAL, Z_FINAL, x_slots, z_slots, xs, xr, zs, zr)
+    g0 = torus.z_arc(lambda t: rx_ref.at[t], first_or_last((2, 2)), g0_slots, g0s, g0r)
+    g1 = torus.z_arc(lambda t: rx1.at[t], first_or_last((2, 2)), g1_slots, g1s, g1r)
+    h0 = torus.x_arc(lambda t: rz_ref.at[t], first_or_last((1, 2)), h0_slots, h0s, h0r)
+    h1 = torus.x_arc(lambda t: rz1.at[t], first_or_last((1, 1)), h1_slots, h1s, h1r)
+
+    links(3, 0, "send")
+    exchange(dq_ref, qpieces, qsend, qrecv, place, False)
+    qpieces[ep] = dq_ref[ep]
+    loads[0].wait()
     total.start()
+    for i in range(4):
+        fetches[i].wait()
+        xa[i].start()
+    links(2, 1, "send")
+
+    gproj = gproj_ref[...].astype(BF16)
+    for d in range(8):
+        for c in range(4):
+            early[d // 4, d % 4, c, :, 0:128] = gproj[32 * c : 32 * c + 32, 128 * d : 128 * d + 128]
+    side = jnp.concatenate([grouter_ref[...], jnp.zeros((96, 1024), F32)], axis=0)
+    for d in range(8):
+        tile = side[:, d * 128 : (d + 1) * 128].T.astype(BF16)
+        for c in range(4):
+            early[d // 4, d % 4, c, :, 128:256] = tile[32 * c : 32 * c + 32]
     total.far()
-    for half in (0, 1):
-        link(0, 2, half, "send")
-        link(1, 1, half, "send")
-    for half in (0, 1):
-        link(0, 1, half, "send")
-        link(1, 2, half, "send")
+    links(1, 2, "send")
+    h0.start()
+    xa[0].advance(2)
     total.near()
+    xa[1].advance(2)
+    sums_early = Direct(torus, early, e_x, e_res, e_z, es, er)
+    sums_late = Direct(torus, late, l_x, l_res, l_z, ls, lr)
+    loads[1].wait()
+    exchange(dq_ref, qpieces, qsend, qrecv, place, True)
+
+    def weights(grad, column):
+        out = mm(nall[...].reshape(1024, 1024), grad.reshape(1024, 128), TN).astype(BF16)
+        for d in range(8):
+            for c in range(4):
+                rows = d * 128 + c * 32
+                late[d // 4, d % 4, c, :, column : column + 128] = out[rows : rows + 32]
+
+    weights(dq_ref[...], 0)
+    loads[2].wait()
+    grad_q = jnp.concatenate([qpieces[p] for p in range(8)], axis=1)
+    grad_normed = mm(grad_q, wq[...], NT)
+    xa[2].advance(2)
+    h0.advance(2)
     for shard in range(4):
         for half in (0, 1):
             link(0, shard, half, "recv")
@@ -751,218 +1070,91 @@
 
     lane = lax.broadcasted_iota(jnp.int32, (TOK, 128), 1)
 
+    @pl.when(ctx == 0)
+    def _():
+        kbuf[0, 0] = jnp.zeros((8, TOK, 128), BF16)
+
+    @pl.when(ctx == 3)
+    def _():
+        kbuf[1, 3] = jnp.zeros((8, TOK, 128), BF16)
+
     def own_block(b, carry):
-        left = jnp.where(ctx > 0, 1.0, 0.0)
-        right = jnp.where(ctx < 3, 1.0, 0.0)
-
-        @pl.when(ctx == 0)
-        def _():
-            kbuf[0, 0, b] = jnp.zeros((TOK, 128), BF16)
-
-        @pl.when(ctx == 3)
-        def _():
-            kbuf[1, 3, b] = jnp.zeros((TOK, 128), BF16)
-
-        grad = dkv_ref[b, ctx].astype(F32) + kbuf[0, ctx, b].astype(F32) * left + kbuf[1, ctx, b].astype(F32) * right
+        grad = dkv_ref[b, ctx].astype(F32) + kbuf[0, ctx, b].astype(F32) + kbuf[1, ctx, b].astype(F32)
         cosine, sine = rope_block(4 * b + ctx, ca_ref, sa_ref, cb_ref, sb_ref)
         cosine = jnp.where(lane < HD, cosine, 1.0)
         sine = jnp.where(lane < HD, sine, 0.0)
-        dqkv[b, :, 0:128] = dq_ref[b]
-        dqkv[b, :, 128:256] = (grad * cosine - rotate_half(grad) * sine).astype(BF16)
+        dkvb[b] = (grad * cosine - rotate_half(grad) * sine).astype(BF16)
         return carry
 
     lax.fori_loop(0, 8, own_block, 0)
-    exchange(dqkv, pieces, psend, precv, place, False)
-    pieces[ep] = dqkv[ep]
-    weights = mm(nall_ref[...].reshape(1024, 1024), dqkv[...].reshape(1024, 256), TN)
-    dense_ref[:, :, 0:256] = weights.astype(BF16).reshape(32, 32, 256)
-    gproj = gproj_ref[...].astype(BF16)
-    for d in range(8):
-        for c in range(4):
-            dense_ref[d * 4 + c, :, 384:512] = gproj[32 * c : 32 * c + 32, 128 * d : 128 * d + 128]
-    out_ref[...] = (res_ref[...] + total.last()).astype(BF16)
-    exchange(dqkv, pieces, psend, precv, place, True)
-    grad_q = jnp.concatenate([pieces[p, :, 0:128] for p in range(8)], axis=1)
-    grad_k = jnp.concatenate([pieces[p, :, 128:192] for p in range(8)], axis=1)
-    grad_v = jnp.concatenate([pieces[p, :, 192:256] for p in range(8)], axis=1)
-    grad_normed = mm(grad_q, wq_ref[...], NT) + mm(grad_k, wk_ref[...], NT) + mm(grad_v, wv_ref[...], NT)
+    exchange(dkvb, kpieces, psend, precv, place, False)
+    kpieces[ep] = dkvb[ep]
+    fetches[4].wait()
+    za[0].start()
+    g0.start()
+    weights(dkvb[...], 128)
+    sums_late.start()
+    sums_early.start()
+    xa[3].advance(2)
+    loads[5].wait()
+    out_ref[...] = (res[...] + total.last()).astype(BF16)
+    for f in (loads[3], loads[4], loads[6]):
+        f.wait()
+    exchange(dkvb, kpieces, psend, precv, place, True)
+    grad_k = jnp.concatenate([kpieces[p, :, 0:HD] for p in range(8)], axis=1)
+    grad_v = jnp.concatenate([kpieces[p, :, HD:128] for p in range(8)], axis=1)
+    grad_normed = grad_normed + mm(grad_k, wk[...], NT) + mm(grad_v, wv[...], NT)
     x = x_ref[...].astype(F32)
     scale = lax.rsqrt(jnp.mean(x * x, axis=-1, keepdims=True) + EPSILON)
     scaled = x * scale
     ggain = jnp.sum(grad_normed * scaled, axis=0, keepdims=True)
+    for t in range(8):
+        gain_own[0, t : t + 1, :] = ggain[:, 128 * t : 128 * t + 128]
+        gain_own[0, 8 + t : 9 + t, :] = ggain_ref[0:1, 128 * t : 128 * t + 128]
+
+    def gain_copy(stage, r):
+        src = gain_own.at[stage]
+        if stage == 0:
+            dst, device, base = gain_e.at[r - 1], (dp, (ep + r) % 8, ctx), 0
+        elif stage == 1:
+            dst, device, base = gain_x.at[r - 1], torus.at_x(torus.x + r), 7
+        else:
+            dst, device, base = gain_z.at[r - 1], torus.at_z(torus.z + r), 10
+        return remote(src, dst, gs.at[base + r], gr.at[base + r], device)
+
+    def gain_stage(stage, count):
+        if stage > 0:
+            last, slots = ((7, gain_e), (3, gain_x), (7, gain_z))[stage - 1]
+            value = gain_own[stage - 1]
+            for r in range(1, last + 1):
+                gain_copy(stage - 1, r).wait_recv()
+                value = value + slots[r - 1]
+            gain_own[stage] = value
+        for r in range(1, count + 1):
+            gain_copy(stage, r).start()
+
+    gain_stage(0, 7)
     grad_normed = grad_normed * gain_ref[...]
     mean = jnp.mean(grad_normed * scaled, axis=-1, keepdims=True)
-    ing_ref[...] = (gres_ref[...] + scale * (grad_normed - scaled * mean)).astype(BF16)
-    side = jnp.concatenate(
-        [grouter_ref[...], jnp.broadcast_to(ggain, (8, 1024)), ggain_ref[...], jnp.zeros((48, 1024), F32)], axis=0
-    )
-    for t in range(8):
-        tile = side[:, t * 128 : (t + 1) * 128].T.astype(BF16)
-        dense_ref[4 * t : 4 * t + 4, :, 256:384] = tile.reshape(4, 32, 128)
-    total.sent()
-    exchange_sent(dqkv, pieces, psend, precv, place)
-    for shard in range(4):
-        for half in (0, 1):
-            for direction in (0, 1):
-                link(direction, shard, half, "sent")
-
-
-class Ring:
-    def __init__(self, n, pos, direction, own, slots, device, send, recv, rows):
-        self.n, self.pos, self.direction, self.own, self.slots = n, pos, direction, own, slots
-        self.device, self.send, self.recv, self.rows = device, send, recv, rows
-
-    def chunk(self, s):
-        if self.direction > 0:
-            return (self.pos + 2 * self.n - 1 - s) % self.n
-        return (self.pos + 1 + s) % self.n
-
-    def copy(self, s):
-        src = self.own(self.chunk(0)) if s == 0 else self.slots.at[s - 1]
-        return remote(src, self.slots.at[s], self.send.at[s], self.recv.at[s], self.device)
-
-    def add(self, s):
-        own = self.own(self.chunk(s))
-        held = self.slots.at[s - 1]
-
-        def one(i, carry):
-            index = self.rows(i)
-            held[index] = (held[index].astype(F32) + own[index].astype(F32)).astype(BF16)
-            return carry
-
-        lax.fori_loop(0, self.count(), one, 0)
-
-    def count(self):
-        c = 1
-        for size in self.slots.shape[1:-2]:
-            c *= size
-        return c
-
-    def step(self, s):
-        if s > 0:
-            self.copy(s - 1).wait_recv()
-            self.add(s)
-        self.copy(s).start()
-
-    def sent(self):
-        for s in range(self.n - 1):
-            self.copy(s).wait_send()
-
-
-def sums_kernel(
-    gw_ref, dense_ref,
-    gin_ref, gout_ref, gq_ref, gk_ref, gv_ref, gside_ref, gproj_ref,
-    xa, za, zb, xb, xd, zd, ra, rb, rd, fin, rq, rp,
-    xas, xar, zas, zar, zbs, zbr, xbs, xbr, xds, xdr, zds, zdr, fsend, frecv, hsend, hrecv,
-):
-    dp, ep, ctx = where_am_i()
-    zh, x = dp // 4, dp % 4
-    z = zh * 4 + ctx
-
-    def at_x(v):
-        return (zh * 4 + v % 4, ep, ctx)
-
-    def at_z(v):
-        v = v % 8
-        return ((v // 4) * 4 + x, ep, v % 4)
-
-    x_up, x_dn = at_x(x + 1), at_x(x + 3)
-    z_up, z_dn = at_z(z + 1), at_z(z + 7)
-
-    def send_to(g, h):
-        return (dp, 2 * ctx + g // 2, 2 * (g % 2) + h), (ep, 2 * ctx + g // 2, 2 * (g % 2) + h)
-
-    def is_me(device):
-        return (device[0] == dp) & (device[1] == ep) & (device[2] == ctx)
-
-    barrier = pltpu.get_barrier_semaphore()
-    for device in (x_up, x_dn, z_up, z_dn):
-        greet(barrier, device)
-    for i in range(8):
-        for device in ((dp, i, ep // 2), (i, dp, ep // 2)):
-
-            @pl.when(jnp.logical_not(is_me(device)))
-            def _():
-                greet(barrier, device)
-
-    waits = 4
-    for g in range(4):
-        for h in range(2):
-            for device in send_to(g, h):
-                waits = waits + jnp.where(is_me(device), 0, 1)
-    pl.semaphore_wait(barrier, waits)
-
-    x4 = lambda i: (i // 4, i % 4)
-    z4 = lambda i: (i,)
-    one = lambda i: ()
-
-    def x_first(ref, result, slots_x, slots_z, up, sems):
-        direction = 1 if up else -1
-        ring_x = Ring(4, x, direction, lambda t: ref.at[:, t], slots_x, x_up if up else x_dn, sems[0], sems[1], x4)
-        ring_z = Ring(8, z, direction, lambda t: result.at[t // 4, t % 4], slots_z, z_up if up else z_dn, sems[2], sems[3], one)
-        return ring_x, ring_z
-
-    def z_first(ref, result, slots_z, slots_x, up, sems):
-        direction = 1 if up else -1
-        ring_z = Ring(8, z, direction, lambda t: ref.at[t // 4, :, t % 4], slots_z, z_up if up else z_dn, sems[0], sems[1], z4)
-        ring_x = Ring(4, x, direction, lambda t: result.at[t], slots_x, x_up if up else x_dn, sems[2], sems[3], one)
-        return ring_z, ring_x
-
-    def settle(ring, result):
-        last = ring.n - 2
-        ring.copy(last).wait_recv()
-        own = ring.own(ring.pos)
-
-        def each(i, carry):
-            index = ring.rows(i)
-            result[index] = (ring.slots.at[last][index].astype(F32) + own[index].astype(F32)).astype(BF16)
-            return carry
-
-        lax.fori_loop(0, ring.count(), each, 0)
-
-    def finish(ring):
-        last = ring.n - 2
-        ring.copy(last).wait_recv()
-        return ring.slots[last].astype(F32) + ring.own(ring.pos)[...].astype(F32)
-
-    a, b, dn = [], [], []
-    for i in range(2):
-        a.append(x_first(gw_ref.at[i], ra.at[i], xa.at[i], za.at[i], i == 0, (xas.at[i], xar.at[i], zas.at[i], zar.at[i])))
-        b.append(z_first(gw_ref.at[2 + i], rb.at[i], zb.at[i], xb.at[i], i == 0, (zbs.at[i], zbr.at[i], xbs.at[i], xbr.at[i])))
-        half = dense_ref.at[:, :, :, pl.ds(16 * i, 16)]
-        dn.append(x_first(half, rd.at[i], xd.at[i], zd.at[i], i == 0, (xds.at[i], xdr.at[i], zds.at[i], zdr.at[i])))
-
-    def both(rings, which, s):
-        for i in range(2):
-            rings[i][which].step(s)
-
-    both(dn, 0, 0)
-    both(a, 0, 0)
-    both(b, 0, 0)
-    both(dn, 0, 1)
-    both(dn, 0, 2)
-    both(b, 0, 1)
-    for i in range(2):
-        settle(dn[i][0], rd.at[i])
-    both(dn, 1, 0)
-    both(a, 0, 1)
-    both(b, 0, 2)
-    both(dn, 1, 1)
-    both(b, 0, 3)
-    both(dn, 1, 2)
-    both(a, 0, 2)
-    both(dn, 1, 3)
-    both(b, 0, 4)
-    both(dn, 1, 4)
-    both(b, 0, 5)
-    both(dn, 1, 5)
-    both(b, 0, 6)
-    both(dn, 1, 6)
-
-    for i in range(2):
-        done = finish(dn[i][1])
-        fin[2 * i] = done[0:8]
-        fin[2 * i + 1] = done[8:16]
+    ing_ref[...] = (gres[...] + scale * (grad_normed - scaled * mean)).astype(BF16)
+
+    za[0].advance(2)
+    g0.advance(2)
+    sums_late.turn()
+    gain_stage(1, 3)
+    sums_early.turn()
+    za[0].advance(3)
+    g0.advance(3)
+
+    def put_rx(index, value, i):
+        rx1[index[0] * 4 + index[1], i] = value.astype(BF16)
+
+    for i in range(4):
+        xa[i].finish(partial(put_rx, i=i))
+    g1.start()
+    gain_stage(2, 7)
+    za[0].advance(4)
+    g0.advance(4)
 
     def piece(g, h, kind, device):
         index = g * 2 + h
@@ -970,7 +1162,7 @@
             return remote(fin.at[g, :, pl.ds(0, 384)], rq.at[ep], fsend.at[index], frecv.at[ep], device)
         return remote(fin.at[g, :, pl.ds(384, 128)], rp.at[dp], hsend.at[index], hrecv.at[dp], device)
 
-    def each_piece(act, own):
+    def each_piece(act, local):
         for g in range(4):
             for h in range(2):
                 for kind in (0, 1):
@@ -980,7 +1172,7 @@
                     def _():
                         act(piece(g, h, kind, device))
 
-                    if own:
+                    if local:
 
                         @pl.when(is_me(device))
                         def _():
@@ -989,26 +1181,52 @@
                             else:
                                 rp[dp] = fin[g, :, 384:512]
 
+    done_late, done_early = sums_late.finish(), sums_early.finish()
+    for g in range(4):
+        rows = slice(8 * g, 8 * g + 8)
+        fin[g, :, 0:256] = done_late[rows]
+        fin[g, :, 256:384] = done_early[rows, 128:256]
+        fin[g, :, 384:512] = done_early[rows, 0:128]
     each_piece(lambda c: c.start(), True)
 
-    for i in range(2):
-        settle(a[i][0], ra.at[i])
-    both(a, 1, 0)
-    for i in range(2):
-        settle(b[i][0], rb.at[i])
-    both(b, 1, 0)
-    both(a, 1, 1)
-    both(b, 1, 1)
-    both(a, 1, 2)
-    both(b, 1, 2)
-    both(a, 1, 3)
-    for i in range(2):
-        done = finish(b[i][1])
-        gin_ref[2 + i] = done[0:32]
-        gout_ref[2 + i] = done[32:48]
-    both(a, 1, 4)
-    both(a, 1, 5)
-    both(a, 1, 6)
+    g1.advance(2)
+
+    def put_unit(units):
+        def put(unit, value):
+            j, u = unit // 3, unit % 3
+            if u < 2:
+                gin_ref[j, 16 * u : 16 * u + 16, :] = value
+            else:
+                gout_ref[j] = value
+
+        return put
+
+    def finish_units(arc, units):
+        for way in (0, 1):
+            arc.copy(way, arc.steps).wait_recv()
+        mine = arc.own(arc.pos)
+        up, down = arc.slots.at[0, arc.steps - 1], arc.slots.at[1, arc.steps - 1]
+        put = put_unit(units)
+        for i, unit in enumerate(units):
+            put(unit, mine[i].astype(F32) + up[i].astype(F32) + down[i].astype(F32))
+
+    finish_units(h0, Z_TURN)
+
+    def put_rz(index, value):
+        for h in (0, 1):
+            rz1[index[0], h] = value[:, 512 * h : 512 * h + 512].astype(BF16)
+
+    za[0].finish(put_rz)
+    h1.start()
+    g1.advance(3)
+    h1.advance(2)
+    finish_units(g0, X_TURN)
+    gain_stage_last = gain_own[2]
+    for r in range(1, 8):
+        gain_copy(2, r).wait_recv()
+        gain_stage_last = gain_stage_last + gain_z[r - 1]
+    gain_own[3] = gain_stage_last
+    g1.advance(4)
 
     for i in range(8):
         for kind, device in enumerate(((dp, i, ep // 2), (i, dp, ep // 2))):
@@ -1016,10 +1234,10 @@
             @pl.when(jnp.logical_not(is_me(device)))
             def _():
                 if kind == 0:
-                    src, dst, sems = fin.at[0, :, pl.ds(0, 384)], rq.at[i], (fsend.at[0], frecv.at[i])
+                    src, dst, pair = fin.at[0, :, pl.ds(0, 384)], rq.at[i], (fsend.at[0], frecv.at[i])
                 else:
-                    src, dst, sems = fin.at[0, :, pl.ds(384, 128)], rp.at[i], (hsend.at[0], hrecv.at[i])
-                remote(src, dst, sems[0], sems[1], device).wait_recv()
+                    src, dst, pair = fin.at[0, :, pl.ds(384, 128)], rp.at[i], (hsend.at[0], hrecv.at[i])
+                remote(src, dst, pair[0], pair[1], device).wait_recv()
 
     odd = ctx % 2 == 1
 
@@ -1033,17 +1251,39 @@
     for i in range(1, 8):
         side = side + rq[i, :, 256:384]
     gside_ref[...] = mine(side)
-    gproj_ref[...] = mine(jnp.concatenate([rp[i] for i in range(8)], axis=1))
-
-    for i in range(2):
-        done = finish(a[i][1])
-        gin_ref[i] = done[0:32]
-        gout_ref[i] = done[32:48]
-    for i in range(2):
-        for rings in (a, b, dn):
-            rings[i][0].sent()
-            rings[i][1].sent()
+    gproj_out[...] = mine(jnp.concatenate([rp[i] for i in range(8)], axis=1))
+    for which in (0, 1):
+        row = jnp.broadcast_to(gain_own[3, pl.ds(8 * which + dp, 1), :], (8, 128))
+        gains_ref[8 * which : 8 * which + 8, :] = pltpu.roll(row, (128 - 16 * ep - 4 * ctx) % 128, 1)
+
+    for way in (0, 1):
+        h1.copy(way, 2).wait_recv()
+    for h in (0, 1):
+        value = rz1[torus.x, h].astype(F32) + h1_slots[0, 1, h].astype(F32) + h1_slots[1, 1, h].astype(F32)
+        gout_ref[2, :, 512 * h : 512 * h + 512] = value
+    finish_units(g1, X_FINAL)
+
+    total.sent()
+    exchange_sent(dq_ref, qpieces, qsend, qrecv, place)
+    exchange_sent(dkvb, kpieces, psend, precv, place)
+    for shard in range(4):
+        for half in (0, 1):
+            for direction in (0, 1):
+                link(direction, shard, half, "sent")
+    for arc in xa + za + [g0, g1, h0, h1]:
+        arc.sent()
+    sums_early.sent()
+    sums_late.sent()
+    for stage, count in ((0, 7), (1, 3), (2, 7)):
+        for r in range(1, count + 1):
+            gain_copy(stage, r).wait_send()
     each_piece(lambda c: c.wait_send(), False)
+
+
+def pack_kernel(*refs):
+    count = len(refs) // 2
+    for src, dst in zip(refs[:count], refs[count:]):
+        dst[...] = src[...]
 
 
 def call(kernel, outs, scratch, args, name, collective=None, **more):
@@ -1119,7 +1359,7 @@
     whole = lambda *shape: pl.BlockSpec(shape, lambda j: (0,) * len(shape))
     sums, back, grad_gates, grad_experts = call(
         expert_kernel,
-        [((8, TOK, 1024), BF16), ((8, TOK, 1024), BF16), ((8, 8, TOK), F32), ((4, 32, 48, 1024), BF16)],
+        [((8, TOK, 1024), BF16), ((8, TOK, 1024), BF16), ((8, 8, TOK), F32), ((12, 32, 16, 1024), BF16)],
         [pltpu.VMEM((4, 8 * CAP, 1024), F32), pltpu.VMEM((4, 8 * CAP, 1024), F32)],
         [ffn_all, grad_all, slots, gates_in, w_expert_in, w_expert_out],
         "experts", grid=(4,),
@@ -1129,16 +1369,27 @@
         ],
         out_specs=[
             whole(8, TOK, 1024), whole(8, TOK, 1024), whole(8, 8, TOK),
-            pl.BlockSpec((1, 32, 48, 1024), lambda j: (j, 0, 0, 0)),
+            pl.BlockSpec((3, 32, 16, 1024), lambda j: (j, 0, 0, 0)),
         ],
     )
+    units = grad_experts.reshape(12, 2, 4, 4, 16, 1024)
     own_ffn = lax.dynamic_index_in_dim(ffn_all, ep, 0, False)
-    grad_mixed, grad_res, grad_router, grad_gain_two = call(
+    hbm = pl.BlockSpec(memory_space=pl.ANY)
+    nx, nz = len(X_TURN), len(Z_TURN)
+    grad_mixed, grad_res, grad_router, grad_gain_two, sums_x, sums_z = call(
         turn_kernel,
-        [((8, TOK, 1024), BF16), ((TOK, 1024), F32), ((64, 1024), F32), ((8, 1024), F32)],
-        [pltpu.VMEM((8, 8, TOK), F32)] + scatter_sum_scratch() + sems(8, 8, 13, 13),
-        [back, grad_gates, gates, residual, own_ffn, out_grad, gain_two, wr_rows],
-        "turn", 3,
+        [
+            ((8, TOK, 1024), BF16), ((TOK, 1024), F32), ((32, 1024), F32), ((8, 1024), F32),
+            ((8, nx, 16, 1024), BF16), ((4, nz, 16, 1024), BF16),
+        ],
+        [pltpu.VMEM((8, 8, TOK), F32)] + scatter_sum_scratch() + sems(8, 8, 13, 13)
+        + [
+            pltpu.VMEM((nx + nz, 2, 4, 4, 16, 1024), BF16),
+            pltpu.VMEM((nx, 2, 2, 2, 4, 16, 1024), BF16), pltpu.VMEM((nz, 2, 4, 4, 16, 1024), BF16),
+        ]
+        + sems(nx + nz, (nx, 2, 2), (nx, 2, 2), (nz, 2, 4), (nz, 2, 4)),
+        [back, grad_gates, gates, residual, own_ffn, out_grad, gain_two, wr_rows, units],
+        "turn", 3, in_specs=[vm] * 8 + [hbm],
     )
     grad_q, grad_kv, grad_proj = call(
         attend_back_kernel,
@@ -1147,38 +1398,51 @@
         [first, query, kv_rows, starts, attended_tall, log_sums, grad_mixed, w_proj_own, *tables],
         "attend_back", in_specs=[sm] + [vm] * 11,
     )
-    layer_output, input_grad, dense = call(
+    fx, fz = len(X_FINAL), len(Z_FINAL)
+    results = call(
         final_kernel,
-        [((TOK, 1024), BF16), ((TOK, 1024), BF16), ((32, 32, 512), BF16)],
-        [pltpu.VMEM((2, 4, 8, TOK, 128), BF16), pltpu.VMEM((8, TOK, 256), BF16), pltpu.VMEM((8, TOK, 256), BF16)]
-        + scatter_sum_scratch() + sems(16, 16, 8, 8),
         [
-            grad_q, grad_kv.reshape(8, 4, TOK, 128), sums, residual, layer_input, gain_one, normed_all,
-            w_query, w_key, w_value, grad_res, *tables, grad_router, grad_gain_two, grad_proj,
-        ],
-        "final", 4,
-    )
-    grad_in, grad_out, out_q, out_k, out_v, side, out_proj = call(
-        sums_kernel,
-        [
-            ((4, 32, 1024), F32), ((4, 16, 1024), F32), ((4, 1024), F32), ((4, 512), F32), ((4, 512), F32),
-            ((4, 128), F32), ((4, 1024), F32),
+            ((TOK, 1024), BF16), ((TOK, 1024), BF16), ((4, 32, 1024), F32), ((4, 16, 1024), F32), ((4, 1024), F32),
+            ((4, 512), F32), ((4, 512), F32), ((4, 128), F32), ((4, 1024), F32), ((16, 128), F32),
         ],
         [
-            pltpu.VMEM((2, 3, 2, 4, 48, 1024), BF16), pltpu.VMEM((2, 7, 48, 1024), BF16),
-            pltpu.VMEM((2, 7, 4, 48, 1024), BF16), pltpu.VMEM((2, 3, 48, 1024), BF16),
-            pltpu.VMEM((2, 3, 2, 4, 16, 512), BF16), pltpu.VMEM((2, 7, 16, 512), BF16),
-            pltpu.VMEM((2, 2, 4, 48, 1024), BF16), pltpu.VMEM((2, 4, 48, 1024), BF16),
-            pltpu.VMEM((2, 2, 4, 16, 512), BF16),
+            pltpu.VMEM((8, TOK, 1024), BF16), pltpu.VMEM((TOK, 1024), F32), pltpu.VMEM((8, TOK, 1024), BF16),
+            pltpu.VMEM((1024, 1024), BF16), pltpu.VMEM((1024, 512), BF16), pltpu.VMEM((1024, 512), BF16),
+            pltpu.VMEM((TOK, 1024), F32),
+            pltpu.VMEM((2, 4, 8, TOK, 128), BF16), pltpu.VMEM((8, TOK, 128), BF16), pltpu.VMEM((8, TOK, 128), BF16),
+            pltpu.VMEM((8, TOK, 128), BF16),
+        ]
+        + scatter_sum_scratch()[:3]
+        + [
+            pltpu.VMEM((fx + fz, 2, 4, 4, 16, 1024), BF16),
+            pltpu.VMEM((fx, 2, 2, 2, 4, 16, 1024), BF16), pltpu.VMEM((fz, 2, 4, 4, 16, 1024), BF16),
+            pltpu.VMEM((2, 4, nx, 16, 1024), BF16), pltpu.VMEM((2, 4, fx, 16, 1024), BF16),
+            pltpu.VMEM((2, 2, nz, 16, 1024), BF16), pltpu.VMEM((2, 2, 2, 16, 512), BF16),
+            pltpu.VMEM((8, fx, 16, 1024), BF16), pltpu.VMEM((4, 2, 16, 512), BF16),
+        ]
+        + [pltpu.VMEM((2, 4, 4, 32, 256), BF16)] * 2
+        + [pltpu.VMEM((3, 2, 4, 32, 256), BF16), pltpu.VMEM((8, 32, 256), BF16), pltpu.VMEM((7, 32, 256), BF16)] * 2
+        + [
+            pltpu.VMEM((4, 16, 128), F32), pltpu.VMEM((7, 16, 128), F32), pltpu.VMEM((3, 16, 128), F32),
+            pltpu.VMEM((7, 16, 128), F32),
             pltpu.VMEM((4, 8, 512), F32), pltpu.VMEM((8, 8, 384), F32), pltpu.VMEM((8, 8, 128), F32),
         ]
-        + sems((2, 3), (2, 3), (2, 7), (2, 7), (2, 7), (2, 7), (2, 3), (2, 3), (2, 3), (2, 3), (2, 7), (2, 7), 8, 8, 8, 8),
-        [grad_experts.reshape(4, 2, 4, 4, 48, 1024), dense.reshape(2, 4, 4, 32, 512)],
-        "sums", 5,
+        + sems(
+            7, 8, 8, 16, 16, 8, 8, 8, 8, fx + fz, (fx, 2, 2), (fx, 2, 2), (fz, 2, 4), (fz, 2, 4),
+            (2, 4), (2, 4), (2, 4), (2, 4), (2, 2), (2, 2), (2, 2), (2, 2), 11, 11, 11, 11, 18, 18, 8, 8, 8, 8,
+        ),
+        [
+            grad_q, grad_kv.reshape(8, 4, TOK, 128), layer_input, gain_one, *tables, grad_router, grad_gain_two,
+            grad_proj, sums_x, sums_z,
+            sums, residual, normed_all, w_query, w_key, w_value, grad_res, units,
+        ],
+        "final", 4, in_specs=[vm] * 13 + [hbm] * 8,
     )
-    router = side[:, :64].reshape(4, 8, 8)[:, :, :4].reshape(4, 32)
+    layer_output, input_grad, grad_in, grad_out, out_q, out_k, out_v, side, out_proj, gains = call(
+        pack_kernel, [(r.shape, r.dtype) for r in results], [], results, "pack"
+    )
     return (
-        layer_output, input_grad, side[:, 64], out_q, out_k, out_v, out_proj, side[:, 72], router, grad_in, grad_out,
+        layer_output, input_grad, gains[0, :4], out_q, out_k, out_v, out_proj, gains[8, :4], side[:, :32], grad_in, grad_out,
     )
 
 

time: 373 us -> 302 us (0.81)
  Pallas kernels: 346 us -> 286 us
  local copies, waits for them, and re-layouts: 21.2 us -> 10.3 us
    pallas_call x8, Pallas kernels: 346 us -> 286 us  [call(): pl.pallas_call(kernel, out_shape=[jax.ShapeDtypeStruct(shape, kind) for s...]
    unnamed x25 -> x11, local copies, waits for them, and re-layouts: 10.6 us -> 1.35 us
where the time goes in v2:
time: 302 us; the launch traced here: 299 us
  Pallas kernels  286 us (95%)
  local copies, waits for them, and re-layouts  10.3 us (3%)
    pallas_call x8, Pallas kernels, call(): pl.pallas_call(kernel, out_shape=[jax.ShapeDtypeStruct(shape, kind) for s...  286 us

profile of v2, /device:TPU:8, one launch (start us, length us, event | category | flops | bytes accessed | tf_op | source)
XLA Modules:
  0.0 299.2 jit_solution(17103339434983839574)
XLA Ops:
  0.6 0.0 copy-start.2
  0.7 0.0 copy-start.3
  0.7 1.2 constant_dynamic-slice_fusion.2
  1.9 1.0 constant_dynamic-slice_fusion.4
  2.9 0.0 copy-start.1
  2.9 1.0 pad_maximum_fusion.w_ref
  3.9 0.0 copy-done.2
  3.9 0.7 copy.33.eid_ref
  4.6 0.5 broadcast.18
  5.1 0.0 copy-done.3
  5.1 0.7 reduce.3
  5.8 0.1 reshape.54.so_ref
  5.9 0.0 copy-start
  5.9 0.7 copy.32
  6.5 0.0 copy-done
  6.6 37.1 %first.1 = (bf16[8,128,1024]{2,1,0:T(8,128)(2,1)}, bf16[8,128,128]{2,1,0:T(8,128)(2,1)}, bf16[8,4,128,128]{3,2,1,0:T(8,128)(2,1)}, bf16[8,128,1024]{2,1,0:T(8,12...) custom-call(bf16[128,1024]{1,0:T(8,128)(2,1)} %x_ref.5, f32[1,1024]{1,0:T(1,128)} %bitcast.39, ...), custom_call_target="tpu_custom_call" | custom-call | tf_op jit(solution)/shard_map/first/pallas_call | solution.py:1294
  43.7 0.7 constant_dynamic-slice_fusion.1
  44.4 0.1 copy.36
  44.5 0.5 and_select_fusion.first_ref
  45.0 18.5 %attend.1 = (bf16[8,128,128]{2,1,0:T(8,128)(2,1)}, f32[8,128,128]{2,1,0:T(8,128)}, f32[8,8,256]{2,1,0:T(8,128)}) custom-call(s32[8]{0:T(128)} %and_select_fusion.first_ref, bf16[8,128,128]{2,1,0:T(8,128)(2,1)} %get-tuple-element.59.q_ref, bf16[4096,128]{1,0:T(8,128)(2,1)} %bitcast.29, f32[32,128]{1,0:T(8,128)} %get-tuple-element.58.start_ref), custom_call_target="tpu_custom_call" | custom-call | tf_op jit(solution)/shard_map/attend/pallas_call | solution.py:1294
  63.5 0.0 copy-done.1
  63.5 0.7 pad_bitcast_fusion.wr_ref
  64.2 25.6 %middle.1 = (f32[128,1024]{1,0:T(8,128)}, bf16[8,128,1024]{2,1,0:T(8,128)(2,1)}, f32[8,8,128]{2,1,0:T(8,128)}, f32[64,128]{1,0:T(8,128)}) custom-call(bf16[8,128,128]{2,1,0:T(8,128)(2,1)} %get-tuple-element.63.att_ref, bf16[128,1024]{1,0:T(8,128)(2,1)} %x_ref.5, f32[1,1024]{1,0:T(1,128)} %bitcast.35, bf16[1024,1024]{1,0:T(8,128)(2,1)} %w_ref.1, ...), custom_call_target="tpu_custom_call" | custom-call | tf_op jit(solution)/shard_map/middle/pallas_call | solution.py:1294
  89.8 28.6 %experts.1 = (bf16[8,128,1024]{2,1,0:T(8,128)(2,1)}, bf16[8,128,1024]{2,1,0:T(8,128)(2,1)}, f32[8,8,128]{2,1,0:T(8,128)}, bf16[12,32,16,1024]{3,2,1,0:T(8,128)(2,1)}) custom-call(bf16[8,128,1024]{2,1,0:T(8,128)(2,1)} %get-tuple-element.65.nf_ref, bf16[8,128,1024]{2,1,0:T(8,128)(2,1)} %get-tuple-element.66.og_ref, f32[8,8,128]{2,1,0:T(8,128)} %get-tuple-element.67.slot_ref, ...), custom_call_target="tpu_custom_call" | custom-call | tf_op jit(solution)/shard_map/experts/pallas_call | solution.py:1294
  118.5 1.7 dynamic-slice_bitcast_fusion.nf_ref
  120.2 45.5 %turn.1 = (bf16[8,128,1024]{2,1,0:T(8,128)(2,1)}, f32[128,1024]{1,0:T(8,128)}, f32[32,1024]{1,0:T(8,128)}, f32[8,1024]{1,0:T(8,128)}, bf16[8,4,16,1024]{3,2,1,0:...) custom-call(bf16[8,128,1024]{2,1,0:T(8,128)(2,1)} %get-tuple-element.69.part_ref, f32[8,8,128]{2,1,0:T(8,128)} %get-tuple-element.70.dg_ref, ...), custom_call_target="tpu_custom_call" | custom-call | tf_op jit(solution)/shard_map/turn/pallas_call | solution.py:1294
  165.7 1.7 constant_dynamic-slice_fusion.w_ref
  167.3 22.2 %attend_back.1 = (bf16[8,128,128]{2,1,0:T(8,128)(2,1)}, bf16[4096,128]{1,0:T(8,128)(2,1)}, f32[128,1024]{1,0:T(8,128)}) custom-call(s32[8]{0:T(128)} %and_select_fusion.first_ref, bf16[8,128,128]{2,1,0:T(8,128)(2,1)} %get-tuple-element.59.q_ref, bf16[4096,128]{1,0:T(8,128)(2,1)} %bitcast.30, f32[32,128]{1,0:T(8,128)} %get-tuple-element.58.start_ref, ...), custom_call_target="tpu_custom_call" | custom-call | tf_op jit(solution)/shard_map/attend_back/pallas_call | solution.py:1294
  189.5 106.0 %final.1 = (bf16[128,1024]{1,0:T(8,128)(2,1)}, bf16[128,1024]{1,0:T(8,128)(2,1)}, f32[4,32,1024]{2,1,0:T(8,128)}, f32[4,16,1024]{2,1,0:T(8,128)}, f32[4,1024]{1,...) custom-call(bf16[8,128,128]{2,1,0:T(8,128)(2,1)} %get-tuple-element., ...), custom_call_target="tpu_custom_call" | custom-call | tf_op jit(solution)/shard_map/final/pallas_call | solution.py:1294
  295.6 2.5 pack.1
  298.0 1.2 slice_bitcast_fusion
  (1 shorter events, 0.0 us)
Async XLA Ops:
  0.6 3.2 %copy-start.2 = (s32[128,8]{0,1:T(8,128)S(1)}, s32[128,8]{0,1:T(8,128)}, u32[]{:S(2)}) copy-start(s32[128,8]{0,1:T(8,128)} %param.29) | copy-start | bytes 12292
  0.7 4.5 %copy-start.3 = (s32[1,1024]{1,0:T(1,128)S(1)}, s32[1,1024]{1,0:T(1,128)}, u32[]{:S(2)}) copy-start(s32[1,1024]{1,0:T(1,128)} %param.30) | copy-start | bytes 12292
  2.9 60.6 %copy-start.1 = (bf16[1024,32]{0,1:T(8,128)(2,1)S(1)}, bf16[1024,32]{0,1:T(8,128)(2,1)}, u32[]{:S(2)}) copy-start(bf16[1024,32]{0,1:T(8,128)(2,1)} %param.25) | copy-start | bytes 196612
  5.9 0.7 copy-start
